TPU v7x, 256 devices: a whole 4x4x8 slice. The times are simulated.
256 devices in a mesh: tile: 32 (over x, z_hi, core), chan: 8 (over y, z_lo).
Axes of the slice: x: 4, y: 4, z: 8 (z_hi: 4, z_lo: 2; z = z_hi * 2 + z_lo), core: 2. Of those that a mesh axis runs over, the one named last changes fastest.
Arguments:
- field: bfloat16 [128, 32, 32, 128], P(None, 'tile', 'chan'), may hold values from -6 to 6
- hidden_fine: bfloat16 [128, 32, 32, 128], P(None, 'tile', 'chan'), may hold values from -3 to 3
- seam_tile: int32 [32, 4], replicated, may hold values from -1 to 31, as said below
- seam_code: int32 [32, 4], replicated, may hold values from 0 to 7, as said below
- corner_tile: int32 [32, 4], replicated, may hold values from -1 to 31, as said below
- corner_cell: int32 [32, 4], replicated, may hold values from 0 to 255, as said below
- pair_list: int32 [32], replicated, may hold values from 0 to 31, as said below
- enc_weight: bfloat16 [9, 128, 128], replicated, may hold values from -0.1875 to 0.1875
- enc_bias: float32 [128], replicated, may hold values from -2 to 2
- gru_input: bfloat16 [9, 3, 128, 128], replicated, may hold values from -0.1875 to 0.1875
- gru_state: bfloat16 [9, 3, 128, 128], replicated, may hold values from -0.1875 to 0.1875
- gru_bias: float32 [2, 3, 128], replicated, may hold values from -3 to 3
- coarse_gain: float32 [128], replicated, may hold values from 0.1 to 1.9
- coarse_shift: float32 [128], replicated, may hold values from -3 to 3
- coarse_weight: bfloat16 [128, 128], replicated, may hold values from -0.5 to 0.5
- dec_weight: bfloat16 [9, 128, 256], replicated, may hold values from -0.125 to 0.125
- dec_bias: float32 [128], replicated, may hold values from -2 to 2
Outputs:
- field_next: bfloat16 [128, 32, 32, 128], P(None, 'tile', 'chan')
- hidden_next: bfloat16 [128, 32, 32, 128], P(None, 'tile', 'chan')
Inputs may be any that keep to these rules, and one draw needn't show every extreme that they name: Tiles sit on a grid of 4 rows and 8 columns, closed along the columns, each stored either upright or turned by half a turn; seam_tile names the tile across each stored side, -1 across the grid's top and bottom rows. `seam_code`: the neighbour's side is top or bottom for a top or bottom side, left or right for a left or right side. `corner_tile`: -1 outside the grid's rows and at grid vertices where only three tiles meet. `corner_cell`: A corner cell of the named tile: 0, 127, 128 or 255; 0 where corner_tile is -1. `pair_list`: A tile in the same grid row; the pairing is mutual and no tile pairs with itself.
All inputs are finite; a program needn't handle non-finite values.
Results may differ from a plain program's by a relative error of at most 0.014.
Values may be sent and summed in bfloat16 or wider, within the bound.
A program may use at most 64 MiB of HBM per device.

v0:
```python
import jax
import jax.numpy as jnp
from jax import lax
from jax.sharding import PartitionSpec as P

PY = 32
PX = 128
STEPS = 2


def padded_2(shard, sides, width):
    for axis, dim in sides:
        peers, length = (lax.axis_size(axis), shard.shape[dim])
        up = [(i, (i + 1) % peers) for i in range(peers - 1)]
        down = [(j, i) for i, j in up]
        last = lax.slice_in_dim(shard, length - width, length, axis=dim)
        leading = lax.slice_in_dim(shard, 0, width, axis=dim)
        before = lax.ppermute(last, axis, up)
        after = lax.ppermute(leading, axis, down)
        shard = jnp.concatenate([before, shard, after], axis=dim)
    return shard


def fold_rims(rim_cells, height, breadth, lists):
    seam_row, code_row, corner_row, cell_row = lists
    depth = rim_cells.shape[0]
    start_sides = (
        jnp.zeros((depth, breadth), jnp.bfloat16),
        jnp.zeros((depth, breadth), jnp.bfloat16),
        jnp.zeros((depth, height), jnp.bfloat16),
        jnp.zeros((depth, height), jnp.bfloat16),
    )
    start_corners = tuple((jnp.zeros((depth, 1), jnp.bfloat16) for corner_id in range(4)))
    pieces = lax.all_gather(rim_cells[None], "tile", axis=0, tiled=True)
    amount = pieces.shape[0]
    new_sides = []
    for side_id in range(4):
        length = breadth if side_id < 2 else height
        offset_in = seam_row[side_id]
        landed = (offset_in >= 0) & (offset_in < amount)
        source_rim = lax.dynamic_index_in_dim(
            pieces, jnp.clip(offset_in, 0, amount - 1), 0, keepdims=False
        )
        their_side = code_row[side_id] // 2
        flipped = code_row[side_id] % 2
        offset = jnp.where(
            their_side < 2, their_side * breadth, 2 * breadth + (their_side - 2) * height
        )
        stepping = jnp.arange(length, dtype=jnp.int32)
        gather_at = jnp.where(flipped == 1, offset + length - 1 - stepping, offset + stepping)
        picked = jnp.take(source_rim, gather_at, axis=1)
        new_sides.append(jnp.where(landed, picked, start_sides[side_id]))
    new_corners = []
    for corner_id in range(4):
        offset_in = corner_row[corner_id]
        landed = (offset_in >= 0) & (offset_in < amount)
        source_rim = lax.dynamic_index_in_dim(
            pieces, jnp.clip(offset_in, 0, amount - 1), 0, keepdims=False
        )
        picked = lax.dynamic_slice_in_dim(source_rim, cell_row[corner_id], 1, 1)
        new_corners.append(jnp.where(landed, picked, start_corners[corner_id]))
    return (tuple(new_sides), tuple(new_corners))


def rows_border(stack_in, lists):
    depth = stack_in.shape[0]
    rows_here = stack_in.shape[1]
    breadth = stack_in.shape[2]
    count = lax.axis_size("chan")
    rank = lax.axis_index("chan")
    height = rows_here * count
    pieces = (
        lax.all_to_all(stack_in[None, :, 0, :], "chan", split_axis=1, concat_axis=0, tiled=True),
        lax.all_to_all(
            stack_in[None, :, rows_here - 1, :], "chan", split_axis=1, concat_axis=0, tiled=True
        ),
        lax.all_to_all(stack_in[None, :, :, 0], "chan", split_axis=1, concat_axis=0, tiled=True),
        lax.all_to_all(
            stack_in[None, :, :, breadth - 1], "chan", split_axis=1, concat_axis=0, tiled=True
        ),
    )
    slice_depth = depth // count
    left_column = jnp.transpose(pieces[2], (1, 0, 2)).reshape(slice_depth, height)
    right_column = jnp.transpose(pieces[3], (1, 0, 2)).reshape(slice_depth, height)
    rim_cells = jnp.concatenate(
        [pieces[0][0], pieces[1][count - 1], left_column, right_column], axis=1
    )
    side_strips, corners = fold_rims(rim_cells, height, breadth, lists)
    whole = (
        lax.all_gather(side_strips[0], "chan", axis=0, tiled=True),
        lax.all_gather(side_strips[1], "chan", axis=0, tiled=True),
        lax.all_gather(side_strips[2], "chan", axis=0, tiled=True),
        lax.all_gather(side_strips[3], "chan", axis=0, tiled=True),
        lax.all_gather(corners[0], "chan", axis=0, tiled=True),
        lax.all_gather(corners[1], "chan", axis=0, tiled=True),
        lax.all_gather(corners[2], "chan", axis=0, tiled=True),
        lax.all_gather(corners[3], "chan", axis=0, tiled=True),
    )
    extended = padded_2(stack_in, (("chan", 1),), 1)
    upper = jnp.where(rank == 0, whole[0], extended[:, 0])
    lower = jnp.where(rank == count - 1, whole[1], extended[:, rows_here + 1])
    middle = jnp.concatenate(
        [upper[:, None], extended[:, 1 : rows_here + 1], lower[:, None]], axis=1
    )
    left_full = jnp.concatenate([whole[4], whole[2], whole[6]], axis=1)
    right_full = jnp.concatenate([whole[5], whole[3], whole[7]], axis=1)
    left_part = lax.dynamic_slice_in_dim(left_full, rank * rows_here, rows_here + 2, 1)
    right_part = lax.dynamic_slice_in_dim(right_full, rank * rows_here, rows_here + 2, 1)
    return jnp.concatenate([left_part[:, :, None], middle, right_part[:, :, None]], axis=2)


def local_conv(weights, inputs, form):
    height = inputs.shape[1] - 2
    breadth = inputs.shape[2] - 2
    summed = None
    for tap_id in range(9):
        shift_row = tap_id // 3
        shift_col = tap_id % 3
        tap_term = jnp.einsum(
            form,
            weights[tap_id],
            inputs[:, shift_row : shift_row + height, shift_col : shift_col + breadth],
            preferred_element_type=jnp.float32,
        )
        summed = tap_term if summed is None else summed + tap_term
    return summed


def pair_joint(local_sums, partner):
    every_tile = lax.all_gather(local_sums[None], "tile", axis=0, tiled=True)
    return local_sums + lax.dynamic_index_in_dim(every_tile, partner, 0, keepdims=False)


def row_steps(state, memory, lists, partner, params):
    (
        enc_weight,
        enc_bias,
        gru_input,
        gru_state,
        gru_bias,
        coarse_gain,
        coarse_shift,
        coarse_weight,
        dec_weight,
        dec_bias,
    ) = params
    all_channels = enc_weight.shape[1]
    rows_here = state.shape[1]
    breadth = state.shape[2]
    biases = gru_bias[:, :, :, None, None]
    for step_id in range(STEPS):
        padded = rows_border(state, lists)
        encoded = jax.nn.gelu(
            local_conv(enc_weight, padded, "oi,iyx->oyx") + enc_bias[:, None, None]
        ).astype(jnp.bfloat16)
        both_padded = rows_border(jnp.concatenate([encoded, memory], axis=0), lists)
        from_input = local_conv(gru_input, both_padded[:all_channels], "goi,iyx->goyx")
        from_state = local_conv(gru_state, both_padded[all_channels:], "goi,iyx->goyx")
        update = jax.nn.sigmoid(from_input[0] + biases[0, 0] + (from_state[0] + biases[1, 0]))
        reset = jax.nn.sigmoid(from_input[1] + biases[0, 1] + (from_state[1] + biases[1, 1]))
        candidate = jnp.tanh(from_input[2] + biases[0, 2] + reset * (from_state[2] + biases[1, 2]))
        memory = ((1.0 - update) * candidate + update * memory.astype(jnp.float32)).astype(
            jnp.bfloat16
        )
        coarse = (
            memory.astype(jnp.float32)
            .reshape(all_channels, rows_here // 2, 2, breadth // 2, 2)
            .sum(axis=(2, 4))
            * 0.25
        )
        slab_sums = jnp.stack([jnp.sum(coarse, axis=(1, 2)), jnp.sum(coarse * coarse, axis=(1, 2))])
        local_sums = lax.psum(slab_sums, "chan")
        joint_sums = pair_joint(local_sums, partner)
        counted = 2 * (PY // 2) * (PX // 2)
        average = joint_sums[0] / counted
        spread = joint_sums[1] / counted - average * average
        scaled = (coarse - average[:, None, None]) * lax.rsqrt(spread + 1e-05)[
            :, None, None
        ] * coarse_gain[:, None, None] + coarse_shift[:, None, None]
        active = jax.nn.gelu(scaled).astype(jnp.bfloat16).reshape(all_channels, -1)
        mixed = jnp.dot(coarse_weight, active, preferred_element_type=jnp.float32)
        lifted = (coarse.reshape(all_channels, -1) + mixed).astype(jnp.bfloat16)
        upsampled = jnp.repeat(
            jnp.repeat(lifted.reshape(all_channels, rows_here // 2, breadth // 2), 2, axis=1),
            2,
            axis=2,
        )
        joined = rows_border(jnp.concatenate([upsampled, memory], axis=0), lists)
        change = local_conv(dec_weight, joined, "oi,iyx->oyx") + dec_bias[:, None, None]
        state = (state.astype(jnp.float32) + change).astype(jnp.bfloat16)
    return (state, memory)


def on_device(
    field,
    hidden_fine,
    seam_tile,
    seam_code,
    corner_tile,
    corner_cell,
    pair_list,
    enc_weight,
    enc_bias,
    gru_input,
    gru_state,
    gru_bias,
    coarse_gain,
    coarse_shift,
    coarse_weight,
    dec_weight,
    dec_bias,
):
    placed = lax.axis_index("tile")
    seam_row = lax.dynamic_index_in_dim(seam_tile, placed, 0, keepdims=False)
    code_row = lax.dynamic_index_in_dim(seam_code, placed, 0, keepdims=False)
    corner_row = lax.dynamic_index_in_dim(corner_tile, placed, 0, keepdims=False)
    cell_row = lax.dynamic_index_in_dim(corner_cell, placed, 0, keepdims=False)
    partner = lax.dynamic_index_in_dim(pair_list, placed, 0, keepdims=False)
    lists = (seam_row, code_row, corner_row, cell_row)
    params = (
        enc_weight,
        enc_bias,
        gru_input,
        gru_state,
        gru_bias,
        coarse_gain,
        coarse_shift,
        coarse_weight,
        dec_weight,
        dec_bias,
    )
    state, memory = row_steps(field[:, 0], hidden_fine[:, 0], lists, partner, params)
    return (state[:, None], memory[:, None])


def solution(mesh):
    placed = (
        P(None, "tile", "chan", None),
        P(None, "tile", "chan", None),
        P(),
        P(),
        P(),
        P(),
        P(),
        P(),
        P(),
        P(),
        P(),
        P(),
        P(),
        P(),
        P(),
        P(),
        P(),
    )
    return jax.shard_map(
        on_device,
        mesh=mesh,
        in_specs=placed,
        out_specs=(P(None, "tile", "chan", None), P(None, "tile", "chan", None)),
        check_vma=False,
    )
```

profile of v0, /device:TPU:64, one launch (start us, length us, event | category | flops | bytes accessed | tf_op | source)
XLA Modules:
  0.0 1573.2 jit_solution(12624420560332572599)
XLA Ops:
  54.3 6.3 all-to-all-start.3
  86.2 42.3 %all-gather = bf16[512,320]{1,0:T(8,128)(2,1)S(1)} all-gather(bf16[16,320]{1,0:T(8,128)(2,1)S(1)} %pad_maximum_fusion.54), channel_id=2, replica_groups=mesh['tile'=32,'chan'=8] {'tile'}, dimensions={0}, use_global_device_ids=true | all-gather | bytes 337920 | tf_op jit(solution)/shard_map/all_gather | solution.py:34
  129.4 28.1 %all_gather.170 = bf16[128,32]{1,0:T(8,128)(2,1)S(1)} all-gather(bf16[16,32]{1,0:T(8,128)(2,1)S(1)} %copy.1078), channel_id=1, replica_groups=mesh['tile'=32,'chan'=8] {'chan'}, dimensions={0}, use_global_device_ids=true | all-gather | bytes 9216 | tf_op jit(solution)/shard_map/all_gather | solution.py:92
  161.4 17.4 %all-reduce.29 = (bf16[128]{0:T(256)(128)(2,1)S(1)}, bf16[128]{0:T(256)(128)(2,1)S(1)}, bf16[128]{0:T(256)(128)(2,1)S(1)}, bf16[128]{0:T(256)(128)(2,1)S(1)}) all-reduce(bf16[128]{0:T(256)(128)(2,1)S(1)} %dynamic-update-slice.1, bf16[128]{0:T(256)(128)(2,1)S(1)} %dynamic-update-slice, ...), channel_id=4, replica_groups=mesh['tile'=32,'chan'=8] {'chan'}, use_global_device_ids=true, to_apply=%add.1 | all-reduce | flops 512 | bytes 2048
  178.9 28.1 %all_gather.175 = bf16[128,32]{1,0:T(8,128)(2,1)S(1)} all-gather(bf16[16,32]{1,0:T(8,128)(2,1)S(1)} %copy.1086), channel_id=1, replica_groups=mesh['tile'=32,'chan'=8] {'chan'}, dimensions={0}, use_global_device_ids=true | all-gather | bytes 9216 | tf_op jit(solution)/shard_map/all_gather | solution.py:93
  207.0 28.1 %all_gather.172 = bf16[128,128]{1,0:T(8,128)(2,1)S(1)} all-gather(bf16[16,128]{1,0:T(8,128)(2,1)S(1)} %bitcast_select_fusion.35), channel_id=1, replica_groups=mesh['tile'=32,'chan'=8] {'chan'}, dimensions={0}, use_global_device_ids=true | all-gather | bytes 36864 | tf_op jit(solution)/shard_map/all_gather | solution.py:90
  235.6 28.1 %all_gather.173 = bf16[128,128]{1,0:T(8,128)(2,1)S(1)} all-gather(bf16[16,128]{1,0:T(8,128)(2,1)S(1)} %bitcast_select_fusion.34), channel_id=1, replica_groups=mesh['tile'=32,'chan'=8] {'chan'}, dimensions={0}, use_global_device_ids=true | all-gather | bytes 36864 | tf_op jit(solution)/shard_map/all_gather | solution.py:91
  300.0 6.5 all-to-all-start.5
  306.6 6.3 all-to-all-done.5
  313.0 46.3 %all-gather.5 = bf16[1024,320]{1,0:T(8,128)(2,1)S(1)} all-gather(bf16[32,320]{1,0:T(8,128)(2,1)S(1)} %pad_maximum_fusion.50), channel_id=7, replica_groups=mesh['tile'=32,'chan'=8] {'tile'}, dimensions={0}, use_global_device_ids=true | all-gather | bytes 675840 | tf_op jit(solution)/shard_map/all_gather | solution.py:34
  360.6 28.2 %all_gather.179 = bf16[256,32]{1,0:T(8,128)(2,1)S(1)} all-gather(bf16[32,32]{1,0:T(8,128)(2,1)S(1)} %copy.1101), channel_id=1, replica_groups=mesh['tile'=32,'chan'=8] {'chan'}, dimensions={0}, use_global_device_ids=true | all-gather | bytes 18432 | tf_op jit(solution)/shard_map/all_gather | solution.py:92
  389.8 17.6 %all-reduce.28 = (bf16[256]{0:T(256)(128)(2,1)S(1)}, bf16[256]{0:T(256)(128)(2,1)S(1)}, bf16[256]{0:T(256)(128)(2,1)S(1)}, bf16[256]{0:T(256)(128)(2,1)S(1)}) all-reduce(bf16[256]{0:T(256)(128)(2,1)S(1)} %dynamic-update-slice.5, bf16[256]{0:T(256)(128)(2,1)S(1)} %dynamic-update-slice.4, ...), channel_id=9, replica_groups=mesh['tile'=32,'chan'=8] {'chan'}, use_global_device_ids=true, to_apply=%add.5 | all-reduce | flops 1024 | bytes 4096
  410.6 28.2 %all_gather.184 = bf16[256,32]{1,0:T(8,128)(2,1)S(1)} all-gather(bf16[32,32]{1,0:T(8,128)(2,1)S(1)} %copy.1113), channel_id=1, replica_groups=mesh['tile'=32,'chan'=8] {'chan'}, dimensions={0}, use_global_device_ids=true | all-gather | bytes 18432 | tf_op jit(solution)/shard_map/all_gather | solution.py:93
  438.9 28.2 %all_gather.181 = bf16[256,128]{1,0:T(8,128)(2,1)S(1)} all-gather(bf16[32,128]{1,0:T(8,128)(2,1)S(1)} %bitcast_select_fusion.28), channel_id=1, replica_groups=mesh['tile'=32,'chan'=8] {'chan'}, dimensions={0}, use_global_device_ids=true | all-gather | bytes 73728 | tf_op jit(solution)/shard_map/all_gather | solution.py:90
  467.7 28.2 %all_gather.182 = bf16[256,128]{1,0:T(8,128)(2,1)S(1)} all-gather(bf16[32,128]{1,0:T(8,128)(2,1)S(1)} %bitcast_select_fusion.27), channel_id=1, replica_groups=mesh['tile'=32,'chan'=8] {'chan'}, dimensions={0}, use_global_device_ids=true | all-gather | bytes 73728 | tf_op jit(solution)/shard_map/all_gather | solution.py:91
  515.5 16.9 %psum.14 = f32[2,128]{1,0:T(2,128)S(1)} all-reduce(f32[2,128]{1,0:T(2,128)S(1)} %pad_maximum_fusion.56), channel_id=1, replica_groups=mesh['tile'=32,'chan'=8] {'chan'}, use_global_device_ids=true, to_apply=%region_3.8 | all-reduce | flops 256 | bytes 2048 | tf_op jit(solution)/shard_map/psum | solution.py:172
  532.4 39.4 %all-gather.32 = f32[32,2,128]{2,1,0:T(2,128)S(1)} all-gather(f32[1,2,128]{2,1,0:T(2,128)S(1)} %bitcast.1292), channel_id=12, replica_groups=mesh['tile'=32,'chan'=8] {'tile'}, dimensions={0}, use_global_device_ids=true | all-gather | bytes 33792 | tf_op jit(solution)/shard_map/all_gather | solution.py:130
  605.7 6.5 all-to-all-start.9
  618.8 43.9 %all-gather.11 = bf16[1024,320]{1,0:T(8,128)(2,1)S(1)} all-gather(bf16[32,320]{1,0:T(8,128)(2,1)S(1)} %pad_maximum_fusion.51), channel_id=13, replica_groups=mesh['tile'=32,'chan'=8] {'tile'}, dimensions={0}, use_global_device_ids=true | all-gather | bytes 675840 | tf_op jit(solution)/shard_map/all_gather | solution.py:34
  663.8 28.4 %all_gather.189 = bf16[256,32]{1,0:T(8,128)(2,1)S(1)} all-gather(bf16[32,32]{1,0:T(8,128)(2,1)S(1)} %copy.1175), channel_id=1, replica_groups=mesh['tile'=32,'chan'=8] {'chan'}, dimensions={0}, use_global_device_ids=true | all-gather | bytes 18432 | tf_op jit(solution)/shard_map/all_gather | solution.py:92
  693.2 17.0 %all-reduce.27 = (bf16[256]{0:T(256)(128)(2,1)S(1)}, bf16[256]{0:T(256)(128)(2,1)S(1)}, bf16[256]{0:T(256)(128)(2,1)S(1)}, bf16[256]{0:T(256)(128)(2,1)S(1)}) all-reduce(bf16[256]{0:T(256)(128)(2,1)S(1)} %dynamic-update-slice.9, bf16[256]{0:T(256)(128)(2,1)S(1)} %dynamic-update-slice.8, ...), channel_id=15, replica_groups=mesh['tile'=32,'chan'=8] {'chan'}, use_global_device_ids=true, to_apply=%add.9 | all-reduce | flops 1024 | bytes 4096
  713.2 28.2 %all_gather.194 = bf16[256,32]{1,0:T(8,128)(2,1)S(1)} all-gather(bf16[32,32]{1,0:T(8,128)(2,1)S(1)} %copy.1187), channel_id=1, replica_groups=mesh['tile'=32,'chan'=8] {'chan'}, dimensions={0}, use_global_device_ids=true | all-gather | bytes 18432 | tf_op jit(solution)/shard_map/all_gather | solution.py:93
  741.5 28.2 %all_gather.191 = bf16[256,128]{1,0:T(8,128)(2,1)S(1)} all-gather(bf16[32,128]{1,0:T(8,128)(2,1)S(1)} %bitcast_select_fusion.24), channel_id=1, replica_groups=mesh['tile'=32,'chan'=8] {'chan'}, dimensions={0}, use_global_device_ids=true | all-gather | bytes 73728 | tf_op jit(solution)/shard_map/all_gather | solution.py:90
  771.7 28.2 %all_gather.192 = bf16[256,128]{1,0:T(8,128)(2,1)S(1)} all-gather(bf16[32,128]{1,0:T(8,128)(2,1)S(1)} %bitcast_select_fusion.23), channel_id=1, replica_groups=mesh['tile'=32,'chan'=8] {'chan'}, dimensions={0}, use_global_device_ids=true | all-gather | bytes 73728 | tf_op jit(solution)/shard_map/all_gather | solution.py:91
  835.0 6.4 all-to-all-start.12
  847.7 40.2 %all-gather.16 = bf16[512,320]{1,0:T(8,128)(2,1)S(1)} all-gather(bf16[16,320]{1,0:T(8,128)(2,1)S(1)} %pad_maximum_fusion.55), channel_id=18, replica_groups=mesh['tile'=32,'chan'=8] {'tile'}, dimensions={0}, use_global_device_ids=true | all-gather | bytes 337920 | tf_op jit(solution)/shard_map/all_gather | solution.py:34
  889.1 28.1 %all_gather.198 = bf16[128,32]{1,0:T(8,128)(2,1)S(1)} all-gather(bf16[16,32]{1,0:T(8,128)(2,1)S(1)} %copy.1215), channel_id=1, replica_groups=mesh['tile'=32,'chan'=8] {'chan'}, dimensions={0}, use_global_device_ids=true | all-gather | bytes 9216 | tf_op jit(solution)/shard_map/all_gather | solution.py:92
  921.1 17.3 %all-reduce.26 = (bf16[128]{0:T(256)(128)(2,1)S(1)}, bf16[128]{0:T(256)(128)(2,1)S(1)}, bf16[128]{0:T(256)(128)(2,1)S(1)}, bf16[128]{0:T(256)(128)(2,1)S(1)}) all-reduce(bf16[128]{0:T(256)(128)(2,1)S(1)} %dynamic-update-slice.13, bf16[128]{0:T(256)(128)(2,1)S(1)} %dynamic-update-slice.12, ...), channel_id=20, replica_groups=mesh['tile'=32,'chan'=8] {'chan'}, use_global_device_ids=true, to_apply=%add.13 | all-reduce | flops 512 | bytes 2048
  938.5 28.1 %all_gather.203 = bf16[128,32]{1,0:T(8,128)(2,1)S(1)} all-gather(bf16[16,32]{1,0:T(8,128)(2,1)S(1)} %copy.1223), channel_id=1, replica_groups=mesh['tile'=32,'chan'=8] {'chan'}, dimensions={0}, use_global_device_ids=true | all-gather | bytes 9216 | tf_op jit(solution)/shard_map/all_gather | solution.py:93
  966.6 28.1 %all_gather.200 = bf16[128,128]{1,0:T(8,128)(2,1)S(1)} all-gather(bf16[16,128]{1,0:T(8,128)(2,1)S(1)} %bitcast_select_fusion.33), channel_id=1, replica_groups=mesh['tile'=32,'chan'=8] {'chan'}, dimensions={0}, use_global_device_ids=true | all-gather | bytes 36864 | tf_op jit(solution)/shard_map/all_gather | solution.py:90
  995.2 28.1 %all_gather.201 = bf16[128,128]{1,0:T(8,128)(2,1)S(1)} all-gather(bf16[16,128]{1,0:T(8,128)(2,1)S(1)} %bitcast_select_fusion.32), channel_id=1, replica_groups=mesh['tile'=32,'chan'=8] {'chan'}, dimensions={0}, use_global_device_ids=true | all-gather | bytes 36864 | tf_op jit(solution)/shard_map/all_gather | solution.py:91
  1065.9 6.3 all-to-all-done.17
  1072.3 44.2 %all-gather.21 = bf16[1024,320]{1,0:T(8,128)(2,1)S(1)} all-gather(bf16[32,320]{1,0:T(8,128)(2,1)S(1)} %pad_maximum_fusion.52), channel_id=23, replica_groups=mesh['tile'=32,'chan'=8] {'tile'}, dimensions={0}, use_global_device_ids=true | all-gather | bytes 675840 | tf_op jit(solution)/shard_map/all_gather | solution.py:34
  1117.6 28.2 %all_gather.207 = bf16[256,32]{1,0:T(8,128)(2,1)S(1)} all-gather(bf16[32,32]{1,0:T(8,128)(2,1)S(1)} %copy.1237), channel_id=1, replica_groups=mesh['tile'=32,'chan'=8] {'chan'}, dimensions={0}, use_global_device_ids=true | all-gather | bytes 18432 | tf_op jit(solution)/shard_map/all_gather | solution.py:92
  1146.8 17.0 %all-reduce.25 = (bf16[256]{0:T(256)(128)(2,1)S(1)}, bf16[256]{0:T(256)(128)(2,1)S(1)}, bf16[256]{0:T(256)(128)(2,1)S(1)}, bf16[256]{0:T(256)(128)(2,1)S(1)}) all-reduce(bf16[256]{0:T(256)(128)(2,1)S(1)} %dynamic-update-slice.17, bf16[256]{0:T(256)(128)(2,1)S(1)} %dynamic-update-slice.16, ...), channel_id=25, replica_groups=mesh['tile'=32,'chan'=8] {'chan'}, use_global_device_ids=true, to_apply=%add.17 | all-reduce | flops 1024 | bytes 4096
  1166.8 28.2 %all_gather.212 = bf16[256,32]{1,0:T(8,128)(2,1)S(1)} all-gather(bf16[32,32]{1,0:T(8,128)(2,1)S(1)} %copy.1249), channel_id=1, replica_groups=mesh['tile'=32,'chan'=8] {'chan'}, dimensions={0}, use_global_device_ids=true | all-gather | bytes 18432 | tf_op jit(solution)/shard_map/all_gather | solution.py:93
  1195.1 28.2 %all_gather.209 = bf16[256,128]{1,0:T(8,128)(2,1)S(1)} all-gather(bf16[32,128]{1,0:T(8,128)(2,1)S(1)} %bitcast_select_fusion.18), channel_id=1, replica_groups=mesh['tile'=32,'chan'=8] {'chan'}, dimensions={0}, use_global_device_ids=true | all-gather | bytes 73728 | tf_op jit(solution)/shard_map/all_gather | solution.py:90
  1224.8 28.2 %all_gather.210 = bf16[256,128]{1,0:T(8,128)(2,1)S(1)} all-gather(bf16[32,128]{1,0:T(8,128)(2,1)S(1)} %bitcast_select_fusion.17), channel_id=1, replica_groups=mesh['tile'=32,'chan'=8] {'chan'}, dimensions={0}, use_global_device_ids=true | all-gather | bytes 73728 | tf_op jit(solution)/shard_map/all_gather | solution.py:91
  1275.9 17.1 %psum.15 = f32[2,128]{1,0:T(2,128)S(1)} all-reduce(f32[2,128]{1,0:T(2,128)S(1)} %pad_maximum_fusion.57), channel_id=1, replica_groups=mesh['tile'=32,'chan'=8] {'chan'}, use_global_device_ids=true, to_apply=%region_7.12 | all-reduce | flops 256 | bytes 2048 | tf_op jit(solution)/shard_map/psum | solution.py:172
  1293.1 39.3 %all-gather.33 = f32[32,2,128]{2,1,0:T(2,128)S(1)} all-gather(f32[1,2,128]{2,1,0:T(2,128)S(1)} %bitcast.1291), channel_id=28, replica_groups=mesh['tile'=32,'chan'=8] {'tile'}, dimensions={0}, use_global_device_ids=true | all-gather | bytes 33792 | tf_op jit(solution)/shard_map/all_gather | solution.py:130
  1375.4 6.6 all-to-all-start.21
  1382.1 6.3 all-to-all-done.21
  1388.5 44.3 %all-gather.27 = bf16[1024,320]{1,0:T(8,128)(2,1)S(1)} all-gather(bf16[32,320]{1,0:T(8,128)(2,1)S(1)} %pad_maximum_fusion.53), channel_id=29, replica_groups=mesh['tile'=32,'chan'=8] {'tile'}, dimensions={0}, use_global_device_ids=true | all-gather | bytes 675840 | tf_op jit(solution)/shard_map/all_gather | solution.py:34
  1434.0 28.2 %all_gather.217 = bf16[256,32]{1,0:T(8,128)(2,1)S(1)} all-gather(bf16[32,32]{1,0:T(8,128)(2,1)S(1)} %copy.1308), channel_id=1, replica_groups=mesh['tile'=32,'chan'=8] {'chan'}, dimensions={0}, use_global_device_ids=true | all-gather | bytes 18432 | tf_op jit(solution)/shard_map/all_gather | solution.py:92
  1463.2 17.0 %all-reduce.24 = (bf16[256]{0:T(256)(128)(2,1)S(1)}, bf16[256]{0:T(256)(128)(2,1)S(1)}, bf16[256]{0:T(256)(128)(2,1)S(1)}, bf16[256]{0:T(256)(128)(2,1)S(1)}) all-reduce(bf16[256]{0:T(256)(128)(2,1)S(1)} %dynamic-update-slice.21, bf16[256]{0:T(256)(128)(2,1)S(1)} %dynamic-update-slice.20, ...), channel_id=31, replica_groups=mesh['tile'=32,'chan'=8] {'chan'}, use_global_device_ids=true, to_apply=%add.21 | all-reduce | flops 1024 | bytes 4096
  1483.2 28.2 %all_gather.222 = bf16[256,32]{1,0:T(8,128)(2,1)S(1)} all-gather(bf16[32,32]{1,0:T(8,128)(2,1)S(1)} %copy.1320), channel_id=1, replica_groups=mesh['tile'=32,'chan'=8] {'chan'}, dimensions={0}, use_global_device_ids=true | all-gather | bytes 18432 | tf_op jit(solution)/shard_map/all_gather | solution.py:93
  1511.5 28.2 %all_gather.219 = bf16[256,128]{1,0:T(8,128)(2,1)S(1)} all-gather(bf16[32,128]{1,0:T(8,128)(2,1)S(1)} %bitcast_select_fusion.14), channel_id=1, replica_groups=mesh['tile'=32,'chan'=8] {'chan'}, dimensions={0}, use_global_device_ids=true | all-gather | bytes 73728 | tf_op jit(solution)/shard_map/all_gather | solution.py:90
  1540.3 28.2 %all_gather.220 = bf16[256,128]{1,0:T(8,128)(2,1)S(1)} all-gather(bf16[32,128]{1,0:T(8,128)(2,1)S(1)} %bitcast_select_fusion.13), channel_id=1, replica_groups=mesh['tile'=32,'chan'=8] {'chan'}, dimensions={0}, use_global_device_ids=true | all-gather | bytes 73728 | tf_op jit(solution)/shard_map/all_gather | solution.py:91
  (688 shorter events, 328.2 us)
Async XLA Ops:
  0.6 571.9 %copy-start = (bf16[128,128]{1,0:T(8,128)(2,1)S(1)}, bf16[128,128]{1,0:T(8,128)(2,1)}, u32[]{:S(2)}) copy-start(bf16[128,128]{1,0:T(8,128)(2,1)} %param.39) | copy-start | bytes 98308
  0.6 42.9 %copy-start.11 = (bf16[128,1,4,128]{3,2,1,0:T(4,128)(2,1)S(1)}, bf16[128,1,4,128]{3,2,1,0:T(4,128)(2,1)}, u32[]{:S(2)}) copy-start(bf16[128,1,4,128]{3,2,1,0:T(4,128)(2,1)} %param.25) | copy-start | bytes 393220
  0.7 43.1 %copy-start.9 = (bf16[128,1,4,128]{3,2,1,0:T(4,128)(2,1)S(1)}, bf16[128,1,4,128]{3,2,1,0:T(4,128)(2,1)}, u32[]{:S(2)}) copy-start(bf16[128,1,4,128]{3,2,1,0:T(4,128)(2,1)} %param.26) | copy-start | bytes 393220
  2.7 51.6 %all-to-all-start.2 = ((bf16[1,128,4]{2,0,1:T(2,128)(2,1)}), bf16[1,128,4]{2,0,1:T(2,128)(2,1)S(1)}, u32[]{:S(2)}, u32[]{:S(2)}) async-start(bf16[1,128,4]{2,0,1:T(2,128)(2,1)} %copy.1069), calls=%async_computation.2 | async-start | bytes 131072 | tf_op jit(solution)/shard_map/all_to_all | solution.py:77
  8.6 226.6 %collective-permute-start = (bf16[128,1,128]{2,0,1:T(8,128)(2,1)S(1)}, bf16[128,1,128]{2,0,1:T(8,128)(2,1)S(1)}, u32[]{:S(2)}, u32[]{:S(2)}) collective-permute-start(bf16[128,1,128]{2,0,1:T(8,128)(2,1)S(1)} %get-tuple-element.154), channel_id=1, source_target_pairs={{0,1},{1,2},{2,3},{3,4},{4,5},{5,6},{6,7},{8,9},{9,10},{10,11},{11... | collective-permute-start | bytes 98312 | tf_op jit(solution)/shard_map/ppermute | solution.py:18
  12.5 251.2 %collective-permute-start.1 = (bf16[128,1,128]{2,0,1:T(8,128)(2,1)S(1)}, bf16[128,1,128]{2,0,1:T(8,128)(2,1)S(1)}, u32[]{:S(2)}, u32[]{:S(2)}) collective-permute-start(bf16[128,1,128]{2,0,1:T(8,128)(2,1)S(1)} %get-tuple-element.156), channel_id=1, source_target_pairs={{1,0},{2,1},{3,2},{4,3},{5,4},{6,5},{7,6},{9,8},{10,9},{11,10},{12... | collective-permute-start | bytes 98312 | tf_op jit(solution)/shard_map/ppermute | solution.py:19
  43.5 85.2 %copy-start.36 = (s32[1024]{0:T(1024)}, s32[1024]{0:T(1024)S(1)}, u32[]{:S(2)}) copy-start(s32[1024]{0:T(1024)S(1)} %pad_clamp_fusion.3) | copy-start | bytes 12292
  43.6 114.2 %copy-start.38 = (s32[1024]{0:T(1024)}, s32[1024]{0:T(1024)S(1)}, u32[]{:S(2)}) copy-start(s32[1024]{0:T(1024)S(1)} %pad_clamp_fusion.2) | copy-start | bytes 12292
  54.3 12.7 all-to-all-start.3
  67.0 9.5 all-to-all-start
  70.4 88.3 %copy-start.40 = (s32[1024]{0:T(1024)}, s32[1024]{0:T(1024)S(1)}, u32[]{:S(2)}) copy-start(s32[1024]{0:T(1024)S(1)} %pad_clamp_fusion.1) | copy-start | bytes 12292
  76.5 9.5 all-to-all-start.1
  79.9 80.8 %copy-start.41 = (s32[1024]{0:T(1024)}, s32[1024]{0:T(1024)S(1)}, u32[]{:S(2)}) copy-start(s32[1024]{0:T(1024)S(1)} %pad_clamp_fusion) | copy-start | bytes 12292
  267.2 10.0 all-to-all-start.6
  277.2 10.6 all-to-all-start.7
  287.8 12.2 all-to-all-start.4
  291.8 204.2 %collective-permute-start.3 = (bf16[256,1,128]{2,0,1:T(8,128)(2,1)S(1)}, bf16[256,1,128]{2,0,1:T(8,128)(2,1)S(1)}, u32[]{:S(2)}, u32[]{:S(2)}) collective-permute-start(bf16[256,1,128]{2,0,1:T(8,128)(2,1)S(1)} %get-tuple-element.142), channel_id=1, source_target_pairs={{1,0},{2,1},{3,2},{4,3},{5,4},{6,5},{7,6},{9,8},{10,9},{11,10},{12... | collective-permute-start | bytes 196616 | tf_op jit(solution)/shard_map/ppermute | solution.py:19
  293.1 174.1 %collective-permute-start.2 = (bf16[256,1,128]{2,0,1:T(8,128)(2,1)S(1)}, bf16[256,1,128]{2,0,1:T(8,128)(2,1)S(1)}, u32[]{:S(2)}, u32[]{:S(2)}) collective-permute-start(bf16[256,1,128]{2,0,1:T(8,128)(2,1)S(1)} %get-tuple-element.143), channel_id=1, source_target_pairs={{0,1},{1,2},{2,3},{3,4},{4,5},{5,6},{6,7},{8,9},{9,10},{10,11},{11... | collective-permute-start | bytes 196616 | tf_op jit(solution)/shard_map/ppermute | solution.py:18
  300.0 12.9 all-to-all-start.5
  574.1 10.1 all-to-all-start.10
  584.1 10.0 all-to-all-start.11
  594.1 11.6 all-to-all-start.8
  597.5 202.4 %collective-permute-start.5 = (bf16[256,1,128]{2,0,1:T(8,128)(2,1)S(1)}, bf16[256,1,128]{2,0,1:T(8,128)(2,1)S(1)}, u32[]{:S(2)}, u32[]{:S(2)}) collective-permute-start(bf16[256,1,128]{2,0,1:T(8,128)(2,1)S(1)} %get-tuple-element.140), channel_id=1, source_target_pairs={{1,0},{2,1},{3,2},{4,3},{5,4},{6,5},{7,6},{9,8},{10,9},{11,10},{12... | collective-permute-start | bytes 196616 | tf_op jit(solution)/shard_map/ppermute | solution.py:19
  598.8 171.0 %collective-permute-start.4 = (bf16[256,1,128]{2,0,1:T(8,128)(2,1)S(1)}, bf16[256,1,128]{2,0,1:T(8,128)(2,1)S(1)}, u32[]{:S(2)}, u32[]{:S(2)}) collective-permute-start(bf16[256,1,128]{2,0,1:T(8,128)(2,1)S(1)} %get-tuple-element.141), channel_id=1, source_target_pairs={{0,1},{1,2},{2,3},{3,4},{4,5},{5,6},{6,7},{8,9},{9,10},{10,11},{11... | collective-permute-start | bytes 196616 | tf_op jit(solution)/shard_map/ppermute | solution.py:18
  605.7 12.9 all-to-all-start.9
  612.3 50.8 %copy-start.37 = (s32[1024]{0:T(1024)S(1)}, s32[1024]{0:T(1024)}, u32[]{:S(2)}) copy-start(s32[1024]{0:T(1024)} %copy-done.36) | copy-start | bytes 12292
  618.6 91.7 %copy-start.39 = (s32[1024]{0:T(1024)S(1)}, s32[1024]{0:T(1024)}, u32[]{:S(2)}) copy-start(s32[1024]{0:T(1024)} %copy-done.38) | copy-start | bytes 12292
  805.2 9.6 all-to-all-start.14
  814.8 9.6 all-to-all-start.15
  824.5 10.5 all-to-all-start.13
  829.3 165.4 %collective-permute-start.6 = (bf16[128,1,128]{2,0,1:T(8,128)(2,1)S(1)}, bf16[128,1,128]{2,0,1:T(8,128)(2,1)S(1)}, u32[]{:S(2)}, u32[]{:S(2)}) collective-permute-start(bf16[128,1,128]{2,0,1:T(8,128)(2,1)S(1)} %get-tuple-element.148), channel_id=1, source_target_pairs={{0,1},{1,2},{2,3},{3,4},{4,5},{5,6},{6,7},{8,9},{9,10},{10,11},{11... | collective-permute-start | bytes 98312 | tf_op jit(solution)/shard_map/ppermute | solution.py:18
  833.1 190.2 %collective-permute-start.7 = (bf16[128,1,128]{2,0,1:T(8,128)(2,1)S(1)}, bf16[128,1,128]{2,0,1:T(8,128)(2,1)S(1)}, u32[]{:S(2)}, u32[]{:S(2)}) collective-permute-start(bf16[128,1,128]{2,0,1:T(8,128)(2,1)S(1)} %get-tuple-element.151), channel_id=1, source_target_pairs={{1,0},{2,1},{3,2},{4,3},{5,4},{6,5},{7,6},{9,8},{10,9},{11,10},{12... | collective-permute-start | bytes 98312 | tf_op jit(solution)/shard_map/ppermute | solution.py:19
  835.0 12.6 all-to-all-start.12
  1027.5 10.0 all-to-all-start.18
  1037.5 10.0 all-to-all-start.19
  1047.5 12.4 all-to-all-start.16
  1051.0 202.0 %collective-permute-start.9 = (bf16[256,1,128]{2,0,1:T(8,128)(2,1)S(1)}, bf16[256,1,128]{2,0,1:T(8,128)(2,1)S(1)}, u32[]{:S(2)}, u32[]{:S(2)}) collective-permute-start(bf16[256,1,128]{2,0,1:T(8,128)(2,1)S(1)} %get-tuple-element.138), channel_id=1, source_target_pairs={{1,0},{2,1},{3,2},{4,3},{5,4},{6,5},{7,6},{9,8},{10,9},{11,10},{12... | collective-permute-start | bytes 196616 | tf_op jit(solution)/shard_map/ppermute | solution.py:19
  1052.3 171.0 %collective-permute-start.8 = (bf16[256,1,128]{2,0,1:T(8,128)(2,1)S(1)}, bf16[256,1,128]{2,0,1:T(8,128)(2,1)}, u32[]{:S(2)}, u32[]{:S(2)}) collective-permute-start(bf16[256,1,128]{2,0,1:T(8,128)(2,1)S(1)} %get-tuple-element.139), channel_id=1, source_target_pairs={{0,1},{1,2},{2,3},{3,4},{4,5},{5,6},{6,7},{8,9},{9,10},{10,11},{11... | collective-permute-start | bytes 196616 | tf_op jit(solution)/shard_map/ppermute | solution.py:18
  1059.9 12.3 all-to-all-start.17
  1274.3 58.1 %copy-start.44 = (f32[128]{0:T(128)S(1)}, f32[128]{0:T(128)}, u32[]{:S(2)}) copy-start(f32[128]{0:T(128)} %param.38) | copy-start | bytes 1540
  1274.3 58.1 %copy-start.46 = (f32[128]{0:T(128)S(1)}, f32[128]{0:T(128)}, u32[]{:S(2)}) copy-start(f32[128]{0:T(128)} %param.37) | copy-start | bytes 1540
  1336.5 10.8 all-to-all-start.22
  1347.2 10.7 all-to-all-start.23
  1357.9 17.5 %all-to-all-start.20 = ((bf16[8,2,2048]{2,1,0:T(2,128)(2,1)}), bf16[8,2,2048]{2,1,0:T(2,128)(2,1)S(1)}, u32[]{:S(2)}, u32[]{:S(2)}) async-start(bf16[8,2,2048]{2,1,0:T(2,128)(2,1)} %reshape.1590), calls=%async_computation.20 | async-start | bytes 131072 | tf_op jit(solution)/shard_map/all_to_all | solution.py:73
  1363.8 204.7 %collective-permute-start.11 = (bf16[256,1,128]{2,0,1:T(8,128)(2,1)}, bf16[256,1,128]{2,0,1:T(8,128)(2,1)S(1)}, u32[]{:S(2)}, u32[]{:S(2)}) collective-permute-start(bf16[256,1,128]{2,0,1:T(8,128)(2,1)} %get-tuple-element.136), channel_id=1, source_target_pairs={{1,0},{2,1},{3,2},{4,3},{5,4},{6,5},{7,6},{9,8},{10,9},{11,10},{12... | collective-permute-start | bytes 196616 | tf_op jit(solution)/shard_map/ppermute | solution.py:19
  1365.9 173.9 %collective-permute-start.10 = (bf16[256,1,128]{2,0,1:T(8,128)(2,1)}, bf16[256,1,128]{2,0,1:T(8,128)(2,1)S(1)}, u32[]{:S(2)}, u32[]{:S(2)}) collective-permute-start(bf16[256,1,128]{2,0,1:T(8,128)(2,1)} %get-tuple-element.137), channel_id=1, source_target_pairs={{0,1},{1,2},{2,3},{3,4},{4,5},{5,6},{6,7},{8,9},{9,10},{10,11},{11... | collective-permute-start | bytes 196616 | tf_op jit(solution)/shard_map/ppermute | solution.py:18
  1375.4 13.0 all-to-all-start.21
  1482.2 86.4 %copy-start.1 = (bf16[128,4,128]{2,0,1:T(8,128)(2,1)S(1)}, bf16[128,4,128]{2,0,1:T(8,128)(2,1)}, u32[]{:S(2)}) copy-start(bf16[128,4,128]{2,0,1:T(8,128)(2,1)} %fusion.129) | copy-start | bytes 393220
  (45 other events, 260.5 us)
where the time goes:
time: 1590 us; the launch traced here: 1570 us
  blocking collectives  1150 us (72%)
  starting transfers between devices  139 us (9%)
  local copies, waits for them, and re-layouts  95.7 us (6%)
  waiting for transfers between devices  93.2 us (6%)
  between operations  40.3 us (3%)
  other arithmetic  29.9 us (2%)
  matrix products  22 us (1%)
    all_gather x6, blocking collectives, fold_rims(): pieces = lax.all_gather(rim_cells[None], 'tile', axis=0, tiled=True)  261 us
    all_gather x6, blocking collectives, rows_border(): lax.all_gather(side_strips[2], 'chan', axis=0, tiled=True)  169 us
    all_gather x6, blocking collectives, rows_border(): lax.all_gather(side_strips[0], 'chan', axis=0, tiled=True)  169 us
    all_gather x6, blocking collectives, rows_border(): lax.all_gather(side_strips[1], 'chan', axis=0, tiled=True)  169 us
    all_gather x6, blocking collectives, rows_border(): lax.all_gather(side_strips[3], 'chan', axis=0, tiled=True)  169 us
    unnamed x6, blocking collectives  103 us
    all_gather x2, blocking collectives, pair_joint(): every_tile = lax.all_gather(local_sums[None], 'tile', axis=0, tiled=True)  78.6 us
    psum x2, blocking collectives, row_steps(): local_sums = lax.psum(slab_sums, 'chan')  34.1 us
  transfers between devices with their start and end apart: 36, of which 18 were waited for; matrix products, arithmetic and copies ran while one was open for 5% of the time, Pallas kernels for 0%

commit v1 on v0

v1 whole, which is shorter than its diff:
```python
import functools
import math

import jax
import jax.numpy as jnp
from jax import lax
from jax.experimental import pallas as pl
from jax.experimental.pallas import tpu as pltpu
from jax.sharding import PartitionSpec as P

STEPS = 2
LANES = 128
ROWS = 4
HALF = 64
F32 = jnp.float32
BF16 = jnp.bfloat16
MESH = pl.DeviceIdType.MESH


def gelu(x):
    inner = math.sqrt(2.0 / math.pi) * (x + 0.044715 * (x * x * x))
    return 0.5 * x * (1.0 + jnp.tanh(inner))


def sigmoid(x):
    return 0.5 + 0.5 * jnp.tanh(0.5 * x)


def flat(value):
    return value.reshape(-1, LANES)


def lane_ids(rows):
    return lax.broadcasted_iota(jnp.int32, (rows, LANES), 1)


def wait_for(ref, sem):
    pltpu.make_async_copy(ref, ref, sem).wait()


def three_parts(value):
    high = value.astype(BF16).astype(F32)
    rest = value - high
    middle = rest.astype(BF16).astype(F32)
    return high, middle, rest - middle


def split_tile(t, nz):
    return lax.div(t, 2 * nz), lax.rem(lax.div(t, 2), nz), lax.rem(t, 2)


class Place:
    def __init__(self, nx, nz, ranks):
        self.nx, self.nz, self.ranks = nx, nz, ranks
        self.t = lax.axis_index("tile")
        self.c = lax.axis_index("chan")
        self.x, self.z, self.k = split_tile(self.t, nz)
        self.i = self.x * 2 + self.k
        self.lines = 2 * nx

    def chan_peer(self, d):
        return lax.rem(self.c + d, self.ranks)

    def line_peer(self, d):
        other = lax.rem(self.i + d, self.lines)
        return lax.div(other, 2) * (2 * self.nz) + self.z * 2 + lax.rem(other, 2)

    def z_peer(self, d):
        other = lax.rem(self.z + d, self.nz)
        return self.x * (2 * self.nz) + other * 2 + self.k


class Round:
    def __init__(self, at, refs, arrays, extra, sel, turn, py):
        (self.cols_src, self.p1, self.r8, self.p3src, self.p3, self.h,
         self.up, self.dn, self.cols, self.upx, self.dnx, self.send, self.recv) = refs
        self.at, self.arrays, self.extra, self.sel, self.turn, self.py = at, arrays, extra, sel, turn, py
        self.a = len(arrays)

    def remote(self, src, dst, send, recv, t, c):
        return pltpu.make_async_remote_copy(
            src_ref=src, dst_ref=dst, send_sem=self.send.at[send], recv_sem=self.recv.at[recv],
            device_id=(t, c), device_id_type=MESH,
        )

    def local(self, src, dst, recv):
        return pltpu.make_async_copy(src, dst, self.recv.at[recv])

    def phase1(self, sums=None):
        at, py, ranks = self.at, self.py, self.at.ranks
        lanes = lane_ids(LANES)
        for a, (rows, deep) in enumerate(self.arrays):
            first, last = deep, rows.shape[0] - 1 - deep

            @pl.when(at.c < ranks - 1)
            def _():
                self.remote(rows.at[last], self.up.at[a], 3, 3, at.t, at.c + 1).start()

            @pl.when(at.c > 0)
            def _():
                self.remote(rows.at[first], self.dn.at[a], 4, 4, at.t, at.c - 1).start()

            @pl.when(at.c == 0)
            def _():
                self.local(rows.at[first, at.c], self.p1.at[ranks, a], 0).start()
                for d in range(1, ranks):
                    to = at.chan_peer(d)
                    self.remote(rows.at[first, to], self.p1.at[ranks, a], 1, 0, at.t, to).start()

            @pl.when(at.c == ranks - 1)
            def _():
                self.local(rows.at[last, at.c], self.p1.at[ranks + 1, a], 0).start()
                for d in range(1, ranks):
                    to = at.chan_peer(d)
                    self.remote(rows.at[last, to], self.p1.at[ranks + 1, a], 2, 0, at.t, to).start()

        for a, (rows, deep) in enumerate(self.arrays):
            each = ROWS // rows.shape[0]
            tile = jnp.zeros((LANES, LANES), F32)
            for q in range(ROWS):
                row = flat(rows[q // each]).astype(F32)
                tile = jnp.where(lanes == q, row[:, deep : deep + 1], tile)
                tile = jnp.where(lanes == LANES - py + q, row[:, LANES - 1 - deep : LANES - deep], tile)
            tile = pltpu.roll(tile, ROWS * at.c, 1)
            if sums is not None and a == self.a - 1:
                parts = three_parts(sums[0]) + three_parts(sums[1])
                for j, part in enumerate(parts):
                    tile = jnp.where(lanes == py + 6 * at.c + j, part, tile)
            self.cols_src[:, a] = tile.astype(BF16).reshape(ranks, -1, LANES)
        self.local(self.cols_src.at[at.c], self.p1.at[at.c], 0).start()
        for d in range(1, ranks):
            to = at.chan_peer(d)
            self.remote(self.cols_src.at[to], self.p1.at[at.c], 0, 0, at.t, to).start()

    def phase2(self, sums=False):
        at, py, ranks = self.at, self.py, self.at.ranks
        wait_for(self.p1, self.recv.at[0])
        self.r8[at.i, 0] = self.p1[ranks]
        self.r8[at.i, 1] = self.p1[ranks + 1]
        for a in range(self.a):
            merged = self.p1[0, a].astype(F32)
            for r in range(1, ranks):
                merged = merged + self.p1[r, a].astype(F32)
            if sums and a == self.a - 1:
                lanes = lane_ids(merged.shape[0])
                held = (lanes >= py) & (lanes < py + 6 * ranks)
                kind = lax.rem(lanes - py + 6 * LANES, 6) < 3
                total = jnp.sum(jnp.where(held & kind, merged, 0.0), axis=1, keepdims=True)
                square = jnp.sum(
                    jnp.where(held & jnp.logical_not(kind), merged, 0.0), axis=1, keepdims=True
                )
                merged = jnp.where(held, 0.0, merged)
                parts = three_parts(total) + three_parts(square)
                for j, part in enumerate(parts):
                    merged = jnp.where(lanes == py + 6 * at.i + j, part, merged)
            self.r8[at.i, 2, a] = merged.astype(BF16)
        for d in range(1, at.lines):
            self.remote(self.r8.at[at.i], self.r8.at[at.i], 5, 1, at.line_peer(d), at.c).start()

    def phase3(self, both, sums=False, deep=False):
        at, py = self.at, self.py
        width = py + 2
        wait_for(self.r8.at[pl.ds(0, at.lines - 1)], self.recv.at[1])
        count = 3 * at.lines
        held = self.r8[...].reshape((count,) + self.r8.shape[2:])
        both[pl.ds(0, count), pl.ds(0, self.a)] = held
        turned = jnp.dot(flat(held), self.turn[...], preferred_element_type=F32)
        both[pl.ds(count, count), pl.ds(0, self.a)] = turned.astype(BF16).reshape(held.shape)
        cut = self.r8.shape[3]
        lanes = lane_ids(self.a * cut).reshape(self.a, cut, LANES)

        def take(d, e):
            index = self.sel[d * 12 + e]
            value = both[jnp.maximum(index, 0), pl.ds(0, self.a)].astype(F32)
            return jnp.where(index >= 0, value, 0.0)

        def shift(value, by):
            return pltpu.roll(value, by % LANES, 2)

        base = jnp.zeros((self.a, cut, LANES), F32)
        if sums:
            gathered = self.r8[0, 2].astype(F32)
            for i in range(1, at.lines):
                gathered = gathered + self.r8[i, 2].astype(F32)
            gathered = shift(gathered, 2 * width - py)
            base = jnp.where((lanes >= 2 * width) & (lanes < 2 * width + 6 * at.lines), gathered, 0.0)

        def partial(d, dst):
            dst[0] = take(d, 0).astype(BF16)
            dst[1] = take(d, 1).astype(BF16)
            tile = base
            left = shift(take(d, 2), 1 + py)
            tile = jnp.where((lanes >= 1) & (lanes <= py), left, tile)
            right = shift(take(d, 3), width + 1)
            tile = jnp.where((lanes > width) & (lanes <= width + py), right, tile)
            for e, lane in ((4, 0), (5, width), (6, py + 1), (7, width + py + 1)):
                value = take(d, e + 4 if deep else e)
                tile = jnp.where(lanes == lane, shift(value, lane), tile)
                if deep:
                    beside = 2 * width + e - 4
                    tile = jnp.where(lanes == beside, shift(value, beside - 1), tile)
            dst[2] = tile.astype(BF16)

        for d in range(1, at.nz):
            partial(d, self.p3src.at[d - 1])
            self.remote(self.p3src.at[d - 1], self.p3.at[at.z], 6, 2, at.z_peer(d), at.c).start()
        partial(0, self.p3.at[at.z])

    def halo_sum(self):
        wait_for(self.p3.at[pl.ds(0, self.at.nz - 1)], self.recv.at[2])
        total = self.p3[0].astype(F32)
        for z in range(1, self.at.nz):
            total = total + self.p3[z].astype(F32)
        return total

    def phase4(self, total, extra=None):
        at, ranks = self.at, self.at.ranks
        for p in range(3):
            for a in range(self.a):
                self.h[p, a] = total[p, a].astype(BF16)
            if extra is not None:
                self.h[p, self.a] = extra[p].astype(BF16)
        self.local(self.h.at[2], self.cols.at[at.c], 5).start()
        for d in range(1, ranks):
            to = at.chan_peer(d)
            self.remote(self.h.at[2], self.cols.at[at.c], 7, 5, at.t, to).start()
        for side, rank, buf, bufx, sem in ((0, 0, self.up, self.upx, 3), (1, ranks - 1, self.dn, self.dnx, 4)):
            pieces = [(self.h.at[side, a], buf.at[a, at.c], 8 + side, sem) for a in range(self.a)]
            if self.extra:
                pieces.append((self.h.at[side, self.a], bufx.at[at.c], 8 + side, sem + 3))

            @pl.when(at.c == rank)
            def _():
                for src, dst, _, recv in pieces:
                    self.local(src, dst, recv).start()

            @pl.when(at.c != rank)
            def _():
                for src, dst, send, recv in pieces:
                    self.remote(src, dst, send, recv, at.t, rank).start()

    def finish(self):
        at = self.at
        wait_for(self.up, self.recv.at[3])
        wait_for(self.dn, self.recv.at[4])
        wait_for(self.cols, self.recv.at[5])
        if self.extra:

            @pl.when(at.c == 0)
            def _():
                wait_for(self.upx, self.recv.at[6])

            @pl.when(at.c == at.ranks - 1)
            def _():
                wait_for(self.dnx, self.recv.at[7])

    def slab_cols(self, a):
        value = flat(self.cols[:, a]).astype(F32)
        return pltpu.roll(value, lax.rem(LANES - ROWS * self.at.c, LANES), 1)

    def drain(self):
        at, ranks = self.at, self.at.ranks
        wait_for(self.p1.at[pl.ds(0, ranks - 1)], self.send.at[0])
        wait_for(self.r8.at[pl.ds(0, at.lines - 1)], self.send.at[5])
        wait_for(self.p3.at[pl.ds(0, at.nz - 1)], self.send.at[6])
        wait_for(self.cols.at[pl.ds(0, ranks - 1)], self.send.at[7])

        @pl.when(at.c == 0)
        def _():
            wait_for(self.p1.at[pl.ds(0, ranks - 1)], self.send.at[1])

        @pl.when(at.c == ranks - 1)
        def _():
            wait_for(self.p1.at[pl.ds(0, ranks - 1)], self.send.at[2])

        @pl.when(at.c < ranks - 1)
        def _():
            wait_for(self.up, self.send.at[3])
            wait_for(self.h.at[1], self.send.at[9])

        @pl.when(at.c > 0)
        def _():
            wait_for(self.dn, self.send.at[4])
            wait_for(self.h.at[0], self.send.at[8])


def round_scratch(a, a4, nx, nz, ranks, cut):
    vm = lambda *shape: pltpu.VMEM(shape + (cut, LANES), BF16)
    return [
        vm(ranks, a),
        vm(ranks + 2, a),
        vm(2 * nx, 3, a),
        vm(nz - 1, 3, a),
        vm(nz, 3, a),
        vm(3, a4),
        vm(a, ranks),
        vm(a, ranks),
        vm(ranks, a4),
        vm(ranks),
        vm(ranks),
        pltpu.SemaphoreType.DMA((10,)),
        pltpu.SemaphoreType.DMA((8,)),
    ]


ROUND_REFS = 13


def put_rows(stack, rows, cols, left_lane, right_lane, slots=None):
    lanes = lane_ids(LANES)
    for q, row in enumerate(rows):
        wide = row.astype(F32)
        here = pl.ds((q if slots is None else slots[q]) * LANES, LANES)
        first, last = left_lane + q, right_lane + q
        left = jnp.where(lanes == 0, cols[:, first : first + 1], pltpu.roll(wide, 1, 1))
        right = jnp.where(lanes == LANES - 1, cols[:, last : last + 1], pltpu.roll(wide, LANES - 1, 1))
        stack[pl.ds(0, LANES), here] = left.astype(BF16)
        stack[pl.ds(LANES, LANES), here] = row.astype(BF16)
        stack[pl.ds(2 * LANES, LANES), here] = right.astype(BF16)


def deep_cols(rnd, at, rows, py):
    width = py + 2
    lanes = lane_ids(LANES)
    near, far = flat(rnd.cols[:, 0]).astype(F32), flat(rnd.cols[:, 1]).astype(F32)

    def place(value):
        left = pltpu.roll(value, lax.rem(2 * LANES + 1 - ROWS * at.c, LANES), 1)
        right = pltpu.roll(value, lax.rem(2 * LANES + HALF + 1 - width - ROWS * at.c, LANES), 1)
        return jnp.where(lanes < HALF, left, right)

    one, two = place(near), place(far)
    top, bottom = at.c == 0, at.c == at.ranks - 1

    def put(tile, lane, value, source, where):
        return jnp.where(lanes == jnp.where(where, lane, -1), value[:, source : source + 1], tile)

    beside = 2 * width
    for base, corner, other in ((0, 0, py + 1), (HALF, width, width + py + 1)):
        n = 0 if base == 0 else 1
        one = put(one, base, far, corner, top)
        one = put(one, base + 7, far, other, bottom)
        two = put(two, base, far, beside + n, top)
        two = put(two, base + 1, near, beside + n, top)
        two = put(two, base + 6, near, beside + 2 + n, bottom)
        two = put(two, base + 7, far, beside + 2 + n, bottom)
    zero = jnp.zeros((LANES, LANES), F32)
    for q, row in enumerate(rows):
        wide = row.astype(F32)
        zero = jnp.where(lanes == q, wide[:, 0:1], zero)
        zero = jnp.where(lanes == HALF + q, wide[:, LANES - 1 :], zero)
    return zero, one, two


def edge_stack(edge, rows, cols, open_vertex):
    zero, one, two = cols
    lanes = lane_ids(LANES)
    hide = lambda tile, lane, n: jnp.where(lanes == jnp.where(open_vertex[n], lane, -1), 0.0, tile)
    upper = hide(hide(one, 2, 0), HALF + 2, 1)
    lower = hide(hide(one, 5, 2), HALF + 5, 3)
    put_rows(edge, rows[:3], upper, 0, HALF, (0, 3, 6))
    put_rows(edge, rows[5:], lower, 5, HALF + 5, (1, 4, 7))
    sides = (
        jnp.where(lanes < HALF, two, zero),
        one,
        jnp.where(lanes < HALF, zero, two),
    )
    for a in range(3):
        for b in range(3):
            tile = pltpu.roll(sides[b], LANES - a, 1) if a else sides[b]
            if a == 0 and b == 2:
                tile = hide(tile, 1, 0)
            if a == 0 and b == 0:
                tile = hide(tile, HALF + 1, 1)
            if a == 2 and b == 2:
                tile = hide(tile, 4, 2)
            if a == 2 and b == 0:
                tile = hide(tile, HALF + 4, 3)
            edge[pl.ds(b * LANES, LANES), pl.ds((3 * a + 2) * LANES, LANES)] = tile.astype(BF16)


def conv_rows(stack, weight, row, gates=None):
    summed = None
    for a in range(3):
        term = jnp.dot(
            weight(a), stack[:, pl.ds((row + a) * LANES, 2 * LANES)], preferred_element_type=F32
        )
        summed = term if summed is None else summed + term
    return summed


def kernel(dims, *refs):
    nx, nz, ranks, py = dims
    names = (
        "field", "hidden", "seam", "code", "corner", "cell", "pair", "enc_w", "gi_w", "gh_w", "dec_w",
        "mix_w", "enc_b", "gru_b", "gain", "shift", "dec_b", "turn", "state_out", "memory_out",
    )
    r = dict(zip(names, refs))
    scratch = list(refs[len(names) :])
    take = lambda n: [scratch.pop(0) for _ in range(n)]
    (we, wi, wh, wdl, wdm, s_state, s_mem, s_enc, s_lift, s_edge, gh, both, sel, wsem, vec) = take(15)
    mems, coarses, states = take(2), take(2), take(1)
    round_refs = [take(ROUND_REFS) for _ in range(4)]
    width = py + 2
    cut = LANES // ranks
    lanes = lane_ids(LANES)
    column = lambda j: vec[:, j : j + 1]

    at = Place(nx, nz, ranks)

    barrier = pltpu.get_barrier_semaphore()
    peers = [(at.t, at.chan_peer(d)) for d in range(1, ranks)]
    peers += [(at.line_peer(d), at.c) for d in range(1, at.lines)]
    peers += [(at.z_peer(d), at.c) for d in range(1, nz)]
    for peer in peers:
        pl.semaphore_signal(barrier, inc=1, device_id=peer, device_id_type=MESH)

    copies = []
    for tap in range(9):
        a, lane = tap // 3, pl.ds(tap % 3 * LANES, LANES)
        copies += [
            pltpu.make_async_copy(r["enc_w"].at[tap], we.at[a, pl.ds(0, LANES), lane], wsem.at[0]),
            pltpu.make_async_copy(r["enc_w"].at[8 - tap], we.at[a, pl.ds(LANES, LANES), lane], wsem.at[0]),
            pltpu.make_async_copy(r["gi_w"].at[tap], wi.at[a, :, :, lane], wsem.at[1]),
            pltpu.make_async_copy(r["gh_w"].at[tap], wh.at[a, :, :, lane], wsem.at[2]),
            pltpu.make_async_copy(r["dec_w"].at[tap, :, pl.ds(0, LANES)], wdl.at[a, :, lane], wsem.at[3]),
            pltpu.make_async_copy(
                r["dec_w"].at[tap, :, pl.ds(LANES, LANES)], wdm.at[a, :, lane], wsem.at[4]
            ),
        ]
    for copy in copies:
        copy.start()

    for d in range(nz):
        dest = at.z_peer(d)
        for side in range(4):
            source = r["seam"][side, dest]
            code = r["code"][side, dest]
            sx, sz, sk = split_tile(jnp.maximum(source, 0), nz)
            piece = lax.div(code, 2) if side < 2 else 2
            index = (lax.rem(code, 2) * at.lines + sx * 2 + sk) * 3 + piece
            sel[d * 12 + side] = jnp.where((source >= 0) & (sz == at.z), index, -1)
        for corner in range(4):
            source = r["corner"][corner, dest]
            cell = r["cell"][corner, dest]
            sx, sz, sk = split_tile(jnp.maximum(source, 0), nz)
            flip = jnp.where(lax.rem(cell, LANES) > 0, 1, 0)
            index = (flip * at.lines + sx * 2 + sk) * 3 + lax.div(cell, LANES)
            sel[d * 12 + 4 + corner] = jnp.where((source >= 0) & (sz == at.z), index, -1)
            row_side, col_side = corner // 2, 2 + corner % 2
            near = r["seam"][row_side, dest]
            turned = lax.rem(r["code"][row_side, dest], 2)
            near_held = jnp.maximum(near, 0)
            hop = lambda table: jnp.where(
                turned == 1, r[table][5 - col_side, near_held], r[table][col_side, near_held]
            )
            source = hop("seam")
            turned = lax.rem(turned + lax.rem(hop("code"), 2), 2)
            theirs = jnp.where(turned == 1, corner, 3 - corner)
            sx, sz, sk = split_tile(jnp.maximum(source, 0), nz)
            index = (lax.rem(theirs, 2) * at.lines + sx * 2 + sk) * 3 + lax.div(theirs, 2)
            sel[d * 12 + 8 + corner] = jnp.where((near >= 0) & (source >= 0) & (sz == at.z), index, -1)

    gru_b = r["gru_b"]
    listed = [
        r["enc_b"][...], gru_b[0, 0:1] + gru_b[0, 1:2], gru_b[1, 0:1] + gru_b[1, 1:2], gru_b[2, 0:1],
        gru_b[2, 1:2], r["gain"][...], r["shift"][...], r["dec_b"][...],
    ]
    vec[...] = jnp.transpose(jnp.concatenate(listed + [jnp.zeros((LANES - 8, LANES), F32)], axis=0))

    pl.semaphore_wait(barrier, len(peers))

    def make_round(n, arrays, extra=False):
        return Round(at, round_refs[n], arrays, extra, sel, r["turn"], py)

    def body_rows(rows, rnd, a):
        return [flat(rnd.up[a])] + [flat(rows[q]) for q in range(ROWS)] + [flat(rnd.dn[a])]

    def close_vertices(cols, left, right):
        for n, lane in enumerate((left, right, left + ROWS + 1, right + ROWS + 1)):
            cols = jnp.where(lanes == jnp.where(open_vertex[n], lane, -1), 0.0, cols)
        return cols

    def stack_rows(rows, rnd, a, stack, vertices=False):
        cols = rnd.slab_cols(a)
        if vertices:
            cols = close_vertices(cols, 0, width)
        put_rows(stack, body_rows(rows, rnd, a), cols, 0, width)

    first_rank, last_rank = at.c == 0, at.c == ranks - 1
    seams = [r["seam"][s, at.t] for s in range(4)]
    corners = [r["corner"][s, at.t] for s in range(4)]
    ranked = (first_rank, first_rank, last_rank, last_rank)
    odd = [lax.rem(r["code"][s, at.t], 2) == 1 for s in range(4)]
    turned_rows = (first_rank & odd[0], last_rank & odd[1])
    turned_cols = jnp.where(lanes < HALF, jnp.where(odd[2], 1, 0), jnp.where(odd[3], 1, 0))
    for n, (lane, cell) in enumerate(((0, 0), (HALF, LANES - 1), (ROWS + 1, LANES), (HALF + ROWS + 1, 2 * LANES - 1))):
        turned_here = jnp.where(r["cell"][n, at.t] == cell, 1, 0)
        turned_cols = jnp.where(lanes == jnp.where(ranked[n], lane, -1), turned_here, turned_cols)
    open_vertex = [rank & (corner < 0) for rank, corner in zip(ranked, corners)]

    def stack_state(rows, rnd):
        body = [flat(rnd.up[1])] + body_rows(rows, rnd, 0) + [flat(rnd.dn[1])]
        cols = deep_cols(rnd, at, body, py)
        put_rows(s_state, body[1:7], close_vertices(cols[1], 1, HALF + 1), 1, HALF + 1)
        edge_stack(s_edge, body, cols, open_vertex)

    def state_conv(gate):
        for n in range(2):
            gh[gate, :, pl.ds(2 * n * LANES, 2 * LANES)] = conv_rows(s_mem, lambda a: wh[a, gate], 2 * n)

    rounds = []
    rnd = make_round(0, [(r["field"], 0), (r["field"], 1), (r["hidden"], 0)])
    rounds.append(rnd)
    rnd.phase1()
    rnd.phase2()
    rnd.phase3(both, deep=True)
    rnd.phase4(rnd.halo_sum())
    rnd.finish()
    stack_state(r["field"], rnd)
    stack_rows(r["hidden"], rnd, 2, s_mem, True)
    wait_for(wh, wsem.at[2])
    for gate in range(3):
        state_conv(gate)
    wait_for(we, wsem.at[0])
    wait_for(wi, wsem.at[1])
    state, memory = r["field"], r["hidden"]

    for step in range(STEPS):
        encoded = []
        for n in range(2):
            acc = gelu(conv_rows(s_state, lambda a: we[a, :LANES], 2 * n) + column(0)).astype(BF16)
            encoded += [acc[:, :LANES], acc[:, LANES:]]
        edge = None
        for a in range(3):
            term = jnp.dot(we[a], s_edge[:, pl.ds(3 * a * LANES, 3 * LANES)], preferred_element_type=F32)
            edge = term if edge is None else edge + term
        bias = column(0)
        pick = lambda n, there: gelu(
            jnp.where(there, edge[LANES:, n * LANES : (n + 1) * LANES], edge[:LANES, n * LANES : (n + 1) * LANES])
            + bias
        )
        above, below, beside = pick(0, turned_rows[0]), pick(1, turned_rows[1]), pick(2, turned_cols > 0)
        above = jnp.where(first_rank & (seams[0] < 0), 0.0, above).astype(BF16)
        below = jnp.where(last_rank & (seams[1] < 0), 0.0, below).astype(BF16)
        beside = jnp.where(lanes < jnp.where(seams[2] < 0, HALF, 0), 0.0, beside)
        beside = jnp.where(lanes >= jnp.where(seams[3] < 0, HALF, LANES), 0.0, beside)
        beside = close_vertices(beside, 0, HALF)
        put_rows(s_enc, [above] + encoded + [below], beside, 0, HALF)

        fresh = mems[step]
        coarse_rows = []
        for n in range(2):
            here = pl.ds(2 * n * LANES, 2 * LANES)
            gate = [conv_rows(s_enc, lambda a: wi[a, g], 2 * n) for g in range(3)]
            update = sigmoid(gate[0] + gh[0, :, here] + column(1))
            reset = sigmoid(gate[1] + gh[1, :, here] + column(2))
            candidate = jnp.tanh(gate[2] + column(3) + reset * (gh[2, :, here] + column(4)))
            pair = None
            for q in range(2):
                cut_row = slice(q * LANES, (q + 1) * LANES)
                before = flat(memory[2 * n + q]).astype(F32)
                after = (1.0 - update[:, cut_row]) * candidate[:, cut_row] + update[:, cut_row] * before
                after = after.astype(BF16)
                fresh[2 * n + q] = after.reshape(fresh.shape[1:])
                after = after.astype(F32)
                pair = after if pair is None else pair + after
            other = jnp.where(lax.rem(lanes, 2) == 0, pltpu.roll(pair, LANES - 1, 1), pltpu.roll(pair, 1, 1))
            coarse_rows.append((pair + other) * 0.25)
        coarse = coarses[step]
        for n in range(2):
            coarse[n] = coarse_rows[n].astype(BF16).reshape(coarse.shape[1:])
        sums = (
            0.5 * jnp.sum(coarse_rows[0] + coarse_rows[1], axis=1, keepdims=True),
            0.5
            * jnp.sum(
                coarse_rows[0] * coarse_rows[0] + coarse_rows[1] * coarse_rows[1], axis=1, keepdims=True
            ),
        )

        rnd = make_round(1 + 2 * step, [(fresh, 0), (coarse, 0)], extra=True)
        rounds.append(rnd)
        rnd.phase1(sums)
        rnd.phase2(True)
        rnd.phase3(both, True)
        total = rnd.halo_sum()
        thin = lane_ids(cut)
        slice_here = pl.ds(pl.multiple_of(at.c * cut, cut), cut)
        gain, shift = vec[slice_here, 5:6], vec[slice_here, 6:7]

        def joint(tile):
            tile = jnp.maximum(tile, 0)
            picked = []
            for one in (tile, r["pair"][tile]):
                tx, tz, tk = split_tile(one, nz)
                lane = thin - (2 * width + 6 * (tx * 2 + tk))
                picked.append((rnd.p3[tz, 2, 1].astype(F32), lane))
            result = []
            for low in (0, 3):
                masked = sum(
                    jnp.where((lane >= low) & (lane < low + 3), value, 0.0) for value, lane in picked
                )
                result.append(jnp.sum(masked, axis=1, keepdims=True))
            counted = 2 * (py // 2) * (LANES // 2)
            average = result[0] / counted
            spread = result[1] / counted - average * average
            return average, lax.rsqrt(spread + 1e-05)

        own = joint(at.t)
        stats = [joint(tile) for tile in seams + corners]

        def norm(value, average, scale):
            return gelu((value - average) * scale * gain + shift)

        extra = []
        for side in range(2):
            value = norm(total[side, 1], *stats[side])
            extra.append(jnp.where(seams[side] >= 0, value, 0.0))
        average = jnp.zeros((cut, LANES), F32)
        scale = jnp.zeros((cut, LANES), F32)
        valid = jnp.zeros((cut, LANES), F32)
        spans = ((2, 1, py), (3, width + 1, py), (4, 0, 1), (5, width, 1), (6, py + 1, 1), (7, width + py + 1, 1))
        for e, begin, length in spans:
            inside = (thin >= begin) & (thin < begin + length)
            average = jnp.where(inside, stats[e][0], average)
            scale = jnp.where(inside, stats[e][1], scale)
            flag = jnp.where((seams + corners)[e] >= 0, 1.0, 0.0)
            valid = jnp.where(inside, flag, valid)
        extra.append(jnp.where(valid > 0.0, norm(total[2, 1], average, scale), 0.0))
        colour = total[2, 1]
        for j, part in enumerate(three_parts(own[0]) + three_parts(own[1])):
            colour = jnp.where(thin == 2 * width + j, part, colour)
        pieces = [[total[p, a] for a in range(2)] for p in range(3)]
        pieces[2][1] = colour
        rnd.phase4_pieces = pieces
        phase4_from(rnd, pieces, extra)
        rnd.finish()

        raw = flat(rnd.cols[:, 1]).astype(F32)
        stat_lane = lanes - 2 * width
        mean = jnp.sum(jnp.where((stat_lane >= 0) & (stat_lane < 3), raw, 0.0), axis=1, keepdims=True)
        inverse = jnp.sum(jnp.where((stat_lane >= 3) & (stat_lane < 6), raw, 0.0), axis=1, keepdims=True)
        wide = lambda value: gelu((value - mean) * inverse * column(5) + column(6))
        top, bottom = flat(rnd.up[1]).astype(F32), flat(rnd.dn[1]).astype(F32)
        active = [
            jnp.where(first_rank, flat(rnd.upx[...]).astype(F32), wide(top)),
            wide(coarse_rows[0]),
            wide(coarse_rows[1]),
            jnp.where(last_rank, flat(rnd.dnx[...]).astype(F32), wide(bottom)),
            rnd.slab_cols(2),
        ]
        base = [top, coarse_rows[0], coarse_rows[1], bottom, rnd.slab_cols(1)]
        lifted = [
            (b + jnp.dot(r["mix_w"][...], v.astype(BF16), preferred_element_type=F32)).astype(BF16)
            for b, v in zip(base, active)
        ]
        body = [lifted[0], lifted[1], lifted[1], lifted[2], lifted[2], lifted[3]]
        put_rows(s_lift, body, lifted[4].astype(F32), 0, width)
        stack_rows(fresh, rnd, 0, s_mem)

        if step == 0:
            wait_for(wdl, wsem.at[3])
            wait_for(wdm, wsem.at[4])
        result = r["state_out"] if step == STEPS - 1 else states[step]
        for n in range(2):
            acc = conv_rows(s_lift, lambda a: wdl[a], 2 * n) + conv_rows(s_mem, lambda a: wdm[a], 2 * n)
            acc = acc + column(7)
            for q in range(2):
                before = flat(state[2 * n + q]).astype(F32)
                after = (before + acc[:, q * LANES : (q + 1) * LANES]).astype(BF16)
                result[2 * n + q] = after.reshape(result.shape[1:])
        state, memory = result, fresh
        if step < STEPS - 1:
            rnd = make_round(2 + 2 * step, [(state, 0), (state, 1)])
            rounds.append(rnd)
            rnd.phase1()
            state_conv(0)
            rnd.phase2()
            state_conv(1)
            rnd.phase3(both, deep=True)
            state_conv(2)
            rnd.phase4(rnd.halo_sum())
            rnd.finish()
            stack_state(state, rnd)

    r["memory_out"][...] = memory[...]
    for rnd in rounds:
        rnd.drain()


def phase4_from(rnd, pieces, extra):
    rnd.phase4(Pieces(pieces), extra)


class Pieces:
    def __init__(self, pieces):
        self.pieces = pieces

    def __getitem__(self, key):
        return self.pieces[key[0]][key[1]]


def on_device(
    nx, nz, ranks, py,
    field, hidden_fine, seam_tile, seam_code, corner_tile, corner_cell, pair_list, enc_weight, enc_bias,
    gru_input, gru_state, gru_bias, coarse_gain, coarse_shift, coarse_weight, dec_weight, dec_bias,
):
    cut = LANES // ranks
    rows = lambda v: jnp.transpose(v[:, 0], (1, 0, 2)).reshape(ROWS, ranks, cut, LANES)
    turn = jnp.asarray(jnp.arange(LANES)[:, None] + jnp.arange(LANES)[None, :] == LANES - 1, BF16)
    vmem, smem, anywhere = (pl.BlockSpec(memory_space=s) for s in (pltpu.VMEM, pltpu.SMEM, pl.ANY))
    slab = (ROWS, ranks, cut, LANES)
    scratch = [
        pltpu.VMEM((3, 2 * LANES, 3 * LANES), BF16),
        pltpu.VMEM((3, 3, LANES, 3 * LANES), BF16),
        pltpu.VMEM((3, 3, LANES, 3 * LANES), BF16),
        pltpu.VMEM((3, LANES, 3 * LANES), BF16),
        pltpu.VMEM((3, LANES, 3 * LANES), BF16),
    ]
    scratch += [pltpu.VMEM((3 * LANES, 6 * LANES), BF16) for _ in range(4)]
    scratch += [pltpu.VMEM((3 * LANES, 9 * LANES), BF16)]
    scratch += [
        pltpu.VMEM((3, LANES, ROWS * LANES), F32),
        pltpu.VMEM((2 * 3 * 2 * nx, 3, cut, LANES), BF16),
        pltpu.SMEM((nz * 12,), jnp.int32),
        pltpu.SemaphoreType.DMA((5,)),
        pltpu.VMEM((LANES, LANES), F32),
    ]
    scratch += [pltpu.VMEM(slab, BF16) for _ in range(2)]
    scratch += [pltpu.VMEM((2, ranks, cut, LANES), BF16) for _ in range(2)]
    scratch += [pltpu.VMEM(slab, BF16)]
    for a, a4 in ((3, 3), (2, 3), (2, 2), (2, 3)):
        scratch += round_scratch(a, a4, nx, nz, ranks, cut)
    state, memory = pl.pallas_call(
        functools.partial(kernel, (nx, nz, ranks, py)),
        out_shape=[jax.ShapeDtypeStruct(slab, BF16)] * 2,
        in_specs=[vmem] * 2 + [smem] * 5 + [anywhere] * 4 + [vmem] * 7,
        out_specs=[vmem] * 2,
        scratch_shapes=scratch,
        compiler_params=pltpu.CompilerParams(
            collective_id=0, has_side_effects=True, vmem_limit_bytes=60 * 2**20
        ),
    )(
        rows(field), rows(hidden_fine), seam_tile.T, seam_code.T, corner_tile.T, corner_cell.T, pair_list,
        enc_weight, gru_input, gru_state, dec_weight, coarse_weight,
        enc_bias[None], jnp.transpose(gru_bias, (1, 0, 2)), coarse_gain[None], coarse_shift[None],
        dec_bias[None], turn,
    )
    back = lambda v: jnp.transpose(v.reshape(ROWS, LANES, LANES), (1, 0, 2))[:, None]
    return back(state), back(memory)


def solution(mesh):
    ranks = mesh.shape["chan"]
    tiles = mesh.shape["tile"]
    nz = 4 if tiles == 32 else 2
    nx = tiles // (2 * nz)
    placed = (P(None, "tile", "chan", None),) * 2
    return jax.shard_map(
        functools.partial(on_device, nx, nz, ranks, ROWS * ranks),
        mesh=mesh,
        in_specs=placed + (P(),) * 15,
        out_specs=placed,
        check_vma=False,
    )
```

time: 1590 us -> 109 us (0.07)
  the two profiles are of different devices: /device:TPU:64 before, /device:TPU:1 now
where the time goes in v1:
time: 109 us
  Pallas kernels  104 us (95%)
  local copies, waits for them, and re-layouts  4.16 us (4%)
    pallas_call x1, Pallas kernels, on_device(): pl.pallas_call(functools.partial(kernel, (nx, nz, ranks, py)), out_shape=...  104 us
    transpose x2, local copies, waits for them, and re-layouts, on_device(): jnp.transpose(v[:, 0], (1, 0, 2)).reshape(ROWS, ranks, cut, LANES)  2.29 us

profile of v1, /device:TPU:1, one launch (start us, length us, event | category | flops | bytes accessed | tf_op | source)
XLA Modules:
  0.0 109.2 jit_solution(7112550624841022314)
XLA Ops:
  0.6 0.6 fusion.refs_17_
  1.3 0.0 copy-start
  1.3 1.6 %copy.19 = bf16[4,128,128]{2,1,0:T(8,128)(2,1)} copy(bf16[4,128,128]{2,0,1:T(4,128)(2,1)} %bitcast.29) | data formatting | bytes 262144 | tf_op jit(solution)/shard_map/transpose | solution.py:709
  2.9 0.0 copy-done
  2.9 0.7 copy.20
  3.6 103.8 %shard_map.176 = (bf16[4,8,16,128]{3,2,1,0:T(8,128)(2,1)}, bf16[4,8,16,128]{3,2,1,0:T(8,128)(2,1)}) custom-call(bf16[4,8,16,128]{3,2,1,0:T(8,128)(2,1)} %bitcast.27, bf16[4,8,16,128]{3,2,1,0:T(8,128)(2,1)} %bitcast.28, s32[4,32]{1,0:T(4,128)} %bitcast.34, s32[4,32]{1,0:T(4,128)} %bitcast.35, s32[4,32]{1,0:T(4,128)} %bitcast.36, s32[4,32]{1,0:T(4,128)} %bitcast.37, ...), custom_call_target="tpu_custom_call" | custom-call | tf_op jit(solution)/shard_map/pallas_call | solution.py:734
  107.4 1.9 %copy_bitcast_fusion = (bf16[128,1,4,128]{3,2,1,0:T(4,128)(2,1)}, bf16[128,1,4,128]{3,2,1,0:T(4,128)(2,1)}) fusion(bf16[4,128,128]{2,1,0:T(8,128)(2,1)} %bitcast.32, bf16[4,128,128]{2,1,0:T(8,128)(2,1)} %bitcast.31), kind=kLoop, calls=%fused_computation | loop fusion | bytes 524288 | tf_op jit(solution)/shard_map/broadcast_in_dim | solution.py:749
Async XLA Ops:
  1.3 1.6 %copy-start = (bf16[128,1,4,128]{3,2,1,0:T(4,128)(2,1)S(1)}, bf16[128,1,4,128]{3,2,1,0:T(4,128)(2,1)}, u32[]{:S(2)}) copy-start(bf16[128,1,4,128]{3,2,1,0:T(4,128)(2,1)} %param.18) | copy-start | bytes 393220

commit v2 on v1

--- a/solution.py
+++ b/solution.py
@@ -66,13 +66,13 @@
         return lax.div(other, 2) * (2 * self.nz) + self.z * 2 + lax.rem(other, 2)
 
     def z_peer(self, d):
-        other = lax.rem(self.z + d, self.nz)
-        return self.x * (2 * self.nz) + other * 2 + self.k
+        z, k = lax.rem(self.z + d // 2, self.nz), lax.rem(self.k + d % 2, 2)
+        return self.x * (2 * self.nz) + z * 2 + k
 
 
 class Round:
     def __init__(self, at, refs, arrays, extra, sel, turn, py):
-        (self.cols_src, self.p1, self.r8, self.p3src, self.p3, self.h,
+        (self.cols_src, self.p1, self.own, self.r8, self.p3src, self.p3, self.h,
          self.up, self.dn, self.cols, self.upx, self.dnx, self.send, self.recv) = refs
         self.at, self.arrays, self.extra, self.sel, self.turn, self.py = at, arrays, extra, sel, turn, py
         self.a = len(arrays)
@@ -86,34 +86,9 @@
     def local(self, src, dst, recv):
         return pltpu.make_async_copy(src, dst, self.recv.at[recv])
 
-    def phase1(self, sums=None):
+    def columns(self, sums=None):
         at, py, ranks = self.at, self.py, self.at.ranks
         lanes = lane_ids(LANES)
-        for a, (rows, deep) in enumerate(self.arrays):
-            first, last = deep, rows.shape[0] - 1 - deep
-
-            @pl.when(at.c < ranks - 1)
-            def _():
-                self.remote(rows.at[last], self.up.at[a], 3, 3, at.t, at.c + 1).start()
-
-            @pl.when(at.c > 0)
-            def _():
-                self.remote(rows.at[first], self.dn.at[a], 4, 4, at.t, at.c - 1).start()
-
-            @pl.when(at.c == 0)
-            def _():
-                self.local(rows.at[first, at.c], self.p1.at[ranks, a], 0).start()
-                for d in range(1, ranks):
-                    to = at.chan_peer(d)
-                    self.remote(rows.at[first, to], self.p1.at[ranks, a], 1, 0, at.t, to).start()
-
-            @pl.when(at.c == ranks - 1)
-            def _():
-                self.local(rows.at[last, at.c], self.p1.at[ranks + 1, a], 0).start()
-                for d in range(1, ranks):
-                    to = at.chan_peer(d)
-                    self.remote(rows.at[last, to], self.p1.at[ranks + 1, a], 2, 0, at.t, to).start()
-
         for a, (rows, deep) in enumerate(self.arrays):
             each = ROWS // rows.shape[0]
             tile = jnp.zeros((LANES, LANES), F32)
@@ -127,6 +102,36 @@
                 for j, part in enumerate(parts):
                     tile = jnp.where(lanes == py + 6 * at.c + j, part, tile)
             self.cols_src[:, a] = tile.astype(BF16).reshape(ranks, -1, LANES)
+
+    def phase1(self, columns=None):
+        at, ranks = self.at, self.at.ranks
+        for a, (rows, deep) in enumerate(self.arrays):
+            first, last = deep, rows.shape[0] - 1 - deep
+
+            @pl.when(at.c < ranks - 1)
+            def _():
+                self.remote(rows.at[last], self.up.at[a], 3, 3, at.t, at.c + 1).start()
+
+            @pl.when(at.c > 0)
+            def _():
+                self.remote(rows.at[first], self.dn.at[a], 4, 4, at.t, at.c - 1).start()
+
+            @pl.when(at.c == 0)
+            def _():
+                self.local(rows.at[first, at.c], self.p1.at[ranks, a], 0).start()
+                for d in range(1, ranks):
+                    to = at.chan_peer(d)
+                    self.remote(rows.at[first, to], self.p1.at[ranks, a], 1, 0, at.t, to).start()
+
+            @pl.when(at.c == ranks - 1)
+            def _():
+                self.local(rows.at[last, at.c], self.p1.at[ranks + 1, a], 0).start()
+                for d in range(1, ranks):
+                    to = at.chan_peer(d)
+                    self.remote(rows.at[last, to], self.p1.at[ranks + 1, a], 2, 0, at.t, to).start()
+
+        if columns is not None:
+            columns()
         self.local(self.cols_src.at[at.c], self.p1.at[at.c], 0).start()
         for d in range(1, ranks):
             to = at.chan_peer(d)
@@ -135,9 +140,9 @@
     def phase2(self, sums=False):
         at, py, ranks = self.at, self.py, self.at.ranks
         wait_for(self.p1, self.recv.at[0])
-        self.r8[at.i, 0] = self.p1[ranks]
-        self.r8[at.i, 1] = self.p1[ranks + 1]
         for a in range(self.a):
+            self.own[a, 0] = self.p1[ranks, a]
+            self.own[a, 1] = self.p1[ranks + 1, a]
             merged = self.p1[0, a].astype(F32)
             for r in range(1, ranks):
                 merged = merged + self.p1[r, a].astype(F32)
@@ -153,31 +158,33 @@
                 parts = three_parts(total) + three_parts(square)
                 for j, part in enumerate(parts):
                     merged = jnp.where(lanes == py + 6 * at.i + j, part, merged)
-            self.r8[at.i, 2, a] = merged.astype(BF16)
+            self.own[a, 2] = merged.astype(BF16)
+        self.local(self.own.at[at.k], self.r8.at[at.i], 1).start()
         for d in range(1, at.lines):
-            self.remote(self.r8.at[at.i], self.r8.at[at.i], 5, 1, at.line_peer(d), at.c).start()
+            to = at.line_peer(d)
+            self.remote(self.own.at[lax.rem(to, 2)], self.r8.at[at.i], 5, 1, to, at.c).start()
 
     def phase3(self, both, sums=False, deep=False):
         at, py = self.at, self.py
         width = py + 2
-        wait_for(self.r8.at[pl.ds(0, at.lines - 1)], self.recv.at[1])
+        wait_for(self.r8, self.recv.at[1])
         count = 3 * at.lines
         held = self.r8[...].reshape((count,) + self.r8.shape[2:])
-        both[pl.ds(0, count), pl.ds(0, self.a)] = held
+        both[pl.ds(0, count)] = held
         turned = jnp.dot(flat(held), self.turn[...], preferred_element_type=F32)
-        both[pl.ds(count, count), pl.ds(0, self.a)] = turned.astype(BF16).reshape(held.shape)
-        cut = self.r8.shape[3]
-        lanes = lane_ids(self.a * cut).reshape(self.a, cut, LANES)
+        both[pl.ds(count, count)] = turned.astype(BF16).reshape(held.shape)
+        cut = self.r8.shape[2]
+        lanes = lane_ids(cut)
 
         def take(d, e):
             index = self.sel[d * 12 + e]
-            value = both[jnp.maximum(index, 0), pl.ds(0, self.a)].astype(F32)
+            value = both[jnp.maximum(index, 0)].astype(F32)
             return jnp.where(index >= 0, value, 0.0)
 
         def shift(value, by):
-            return pltpu.roll(value, by % LANES, 2)
-
-        base = jnp.zeros((self.a, cut, LANES), F32)
+            return pltpu.roll(value, by % LANES, 1)
+
+        base = jnp.zeros((cut, LANES), F32)
         if sums:
             gathered = self.r8[0, 2].astype(F32)
             for i in range(1, at.lines):
@@ -201,16 +208,20 @@
                     tile = jnp.where(lanes == beside, shift(value, beside - 1), tile)
             dst[2] = tile.astype(BF16)
 
-        for d in range(1, at.nz):
+        slot = at.z * 2 + at.k
+        for d in reversed(range(1, 2 * at.nz)):
             partial(d, self.p3src.at[d - 1])
-            self.remote(self.p3src.at[d - 1], self.p3.at[at.z], 6, 2, at.z_peer(d), at.c).start()
-        partial(0, self.p3.at[at.z])
+            self.remote(self.p3src.at[d - 1], self.p3.at[slot], 6, 2, at.z_peer(d), at.c).start()
+        partial(0, self.p3.at[slot])
 
     def halo_sum(self):
-        wait_for(self.p3.at[pl.ds(0, self.at.nz - 1)], self.recv.at[2])
-        total = self.p3[0].astype(F32)
-        for z in range(1, self.at.nz):
-            total = total + self.p3[z].astype(F32)
+        wait_for(self.p3.at[pl.ds(0, 2 * self.at.nz - 1)], self.recv.at[2])
+        total = {}
+        for p in range(3):
+            for a in range(self.a):
+                total[p, a] = self.p3[a, p].astype(F32)
+                for z in range(1, self.at.nz):
+                    total[p, a] = total[p, a] + self.p3[2 * z + a, p].astype(F32)
         return total
 
     def phase4(self, total, extra=None):
@@ -262,7 +273,7 @@
         at, ranks = self.at, self.at.ranks
         wait_for(self.p1.at[pl.ds(0, ranks - 1)], self.send.at[0])
         wait_for(self.r8.at[pl.ds(0, at.lines - 1)], self.send.at[5])
-        wait_for(self.p3.at[pl.ds(0, at.nz - 1)], self.send.at[6])
+        wait_for(self.p3.at[pl.ds(0, 2 * at.nz - 1)], self.send.at[6])
         wait_for(self.cols.at[pl.ds(0, ranks - 1)], self.send.at[7])
 
         @pl.when(at.c == 0)
@@ -289,9 +300,10 @@
     return [
         vm(ranks, a),
         vm(ranks + 2, a),
-        vm(2 * nx, 3, a),
-        vm(nz - 1, 3, a),
-        vm(nz, 3, a),
+        vm(a, 3),
+        vm(2 * nx, 3),
+        vm(2 * nz - 1, 3),
+        vm(2 * nz, 3),
         vm(3, a4),
         vm(a, ranks),
         vm(a, ranks),
@@ -303,7 +315,7 @@
     ]
 
 
-ROUND_REFS = 13
+ROUND_REFS = 14
 
 
 def put_rows(stack, rows, cols, left_lane, right_lane, slots=None):
@@ -393,14 +405,19 @@
     nx, nz, ranks, py = dims
     names = (
         "field", "hidden", "seam", "code", "corner", "cell", "pair", "enc_w", "gi_w", "gh_w", "dec_w",
-        "mix_w", "enc_b", "gru_b", "gain", "shift", "dec_b", "turn", "state_out", "memory_out",
+        "mix_w", "enc_b", "gru_b", "gain", "shift", "dec_b", "state_out", "memory_out",
     )
     r = dict(zip(names, refs))
+    given = dict(r)
     scratch = list(refs[len(names) :])
     take = lambda n: [scratch.pop(0) for _ in range(n)]
     (we, wi, wh, wdl, wdm, s_state, s_mem, s_enc, s_lift, s_edge, gh, both, sel, wsem, vec) = take(15)
     mems, coarses, states = take(2), take(2), take(1)
-    round_refs = [take(ROUND_REFS) for _ in range(4)]
+    field, hidden, turn = take(3)
+    loaded = ("field", "hidden", "seam", "code", "corner", "cell", "pair", "mix_w", "enc_b", "gru_b", "gain", "shift", "dec_b")
+    held = take(len(loaded))
+    (lsem,) = take(1)
+    round_refs = [take(ROUND_REFS) for _ in range(5)]
     width = py + 2
     cut = LANES // ranks
     lanes = lane_ids(LANES)
@@ -411,7 +428,7 @@
     barrier = pltpu.get_barrier_semaphore()
     peers = [(at.t, at.chan_peer(d)) for d in range(1, ranks)]
     peers += [(at.line_peer(d), at.c) for d in range(1, at.lines)]
-    peers += [(at.z_peer(d), at.c) for d in range(1, nz)]
+    peers += [(at.z_peer(d), at.c) for d in range(2, 2 * nz)]
     for peer in peers:
         pl.semaphore_signal(barrier, inc=1, device_id=peer, device_id_type=MESH)
 
@@ -428,10 +445,17 @@
                 r["dec_w"].at[tap, :, pl.ds(LANES, LANES)], wdm.at[a, :, lane], wsem.at[4]
             ),
         ]
+    loads = {}
+    for n, name in enumerate(loaded):
+        r[name] = held[n]
+        loads[name] = pltpu.make_async_copy(given[name], held[n], lsem.at[n])
+        loads[name].start()
     for copy in copies:
         copy.start()
-
-    for d in range(nz):
+    for name in loaded[2:7]:
+        loads[name].wait()
+
+    for d in range(2 * nz):
         dest = at.z_peer(d)
         for side in range(4):
             source = r["seam"][side, dest]
@@ -461,6 +485,15 @@
             index = (lax.rem(theirs, 2) * at.lines + sx * 2 + sk) * 3 + lax.div(theirs, 2)
             sel[d * 12 + 8 + corner] = jnp.where((near >= 0) & (source >= 0) & (sz == at.z), index, -1)
 
+    for name, rows in (("field", field), ("hidden", hidden)):
+        loads[name].wait()
+        wide = r[name][...].astype(F32)
+        for q in range(ROWS):
+            rows[q] = wide[:, q, :].astype(BF16).reshape(rows.shape[1:])
+    turn[...] = jnp.where(lanes + lax.broadcasted_iota(jnp.int32, (LANES, LANES), 0) == LANES - 1, 1.0, 0.0).astype(BF16)
+
+    for name in loaded[7:]:
+        loads[name].wait()
     gru_b = r["gru_b"]
     listed = [
         r["enc_b"][...], gru_b[0, 0:1] + gru_b[0, 1:2], gru_b[1, 0:1] + gru_b[1, 1:2], gru_b[2, 0:1],
@@ -468,10 +501,8 @@
     ]
     vec[...] = jnp.transpose(jnp.concatenate(listed + [jnp.zeros((LANES - 8, LANES), F32)], axis=0))
 
-    pl.semaphore_wait(barrier, len(peers))
-
     def make_round(n, arrays, extra=False):
-        return Round(at, round_refs[n], arrays, extra, sel, r["turn"], py)
+        return Round(at, round_refs[n], arrays, extra, sel, turn, py)
 
     def body_rows(rows, rnd, a):
         return [flat(rnd.up[a])] + [flat(rows[q]) for q in range(ROWS)] + [flat(rnd.dn[a])]
@@ -509,24 +540,7 @@
         for n in range(2):
             gh[gate, :, pl.ds(2 * n * LANES, 2 * LANES)] = conv_rows(s_mem, lambda a: wh[a, gate], 2 * n)
 
-    rounds = []
-    rnd = make_round(0, [(r["field"], 0), (r["field"], 1), (r["hidden"], 0)])
-    rounds.append(rnd)
-    rnd.phase1()
-    rnd.phase2()
-    rnd.phase3(both, deep=True)
-    rnd.phase4(rnd.halo_sum())
-    rnd.finish()
-    stack_state(r["field"], rnd)
-    stack_rows(r["hidden"], rnd, 2, s_mem, True)
-    wait_for(wh, wsem.at[2])
-    for gate in range(3):
-        state_conv(gate)
-    wait_for(we, wsem.at[0])
-    wait_for(wi, wsem.at[1])
-    state, memory = r["field"], r["hidden"]
-
-    for step in range(STEPS):
+    def encode():
         encoded = []
         for n in range(2):
             acc = gelu(conv_rows(s_state, lambda a: we[a, :LANES], 2 * n) + column(0)).astype(BF16)
@@ -548,6 +562,38 @@
         beside = close_vertices(beside, 0, HALF)
         put_rows(s_enc, [above] + encoded + [below], beside, 0, HALF)
 
+    rounds = []
+    rnd = make_round(0, [(field, 0), (field, 1)])
+    late = make_round(4, [(hidden, 0), (hidden, 1)])
+    rounds += [rnd, late]
+    rnd.columns()
+    late.columns()
+
+    pl.semaphore_wait(barrier, len(peers))
+
+    rnd.phase1()
+    late.phase1()
+    rnd.phase2()
+    late.phase2()
+    rnd.phase3(both, deep=True)
+    late.phase3(both, deep=True)
+    rnd.phase4(rnd.halo_sum())
+    late.phase4(late.halo_sum())
+    rnd.finish()
+    stack_state(field, rnd)
+    wait_for(we, wsem.at[0])
+    encode()
+    late.finish()
+    stack_rows(hidden, late, 0, s_mem, True)
+    wait_for(wh, wsem.at[2])
+    for gate in range(3):
+        state_conv(gate)
+    wait_for(wi, wsem.at[1])
+    state, memory = field, hidden
+
+    for step in range(STEPS):
+        if step > 0:
+            encode()
         fresh = mems[step]
         coarse_rows = []
         for n in range(2):
@@ -580,7 +626,7 @@
 
         rnd = make_round(1 + 2 * step, [(fresh, 0), (coarse, 0)], extra=True)
         rounds.append(rnd)
-        rnd.phase1(sums)
+        rnd.phase1(lambda: rnd.columns(sums))
         rnd.phase2(True)
         rnd.phase3(both, True)
         total = rnd.halo_sum()
@@ -594,7 +640,7 @@
             for one in (tile, r["pair"][tile]):
                 tx, tz, tk = split_tile(one, nz)
                 lane = thin - (2 * width + 6 * (tx * 2 + tk))
-                picked.append((rnd.p3[tz, 2, 1].astype(F32), lane))
+                picked.append((rnd.p3[2 * tz + 1, 2].astype(F32), lane))
             result = []
             for low in (0, 3):
                 masked = sum(
@@ -630,10 +676,8 @@
         colour = total[2, 1]
         for j, part in enumerate(three_parts(own[0]) + three_parts(own[1])):
             colour = jnp.where(thin == 2 * width + j, part, colour)
-        pieces = [[total[p, a] for a in range(2)] for p in range(3)]
-        pieces[2][1] = colour
-        rnd.phase4_pieces = pieces
-        phase4_from(rnd, pieces, extra)
+        total[2, 1] = colour
+        rnd.phase4(total, extra)
         rnd.finish()
 
         raw = flat(rnd.cols[:, 1]).astype(F32)
@@ -673,7 +717,7 @@
         if step < STEPS - 1:
             rnd = make_round(2 + 2 * step, [(state, 0), (state, 1)])
             rounds.append(rnd)
-            rnd.phase1()
+            rnd.phase1(rnd.columns)
             state_conv(0)
             rnd.phase2()
             state_conv(1)
@@ -688,27 +732,13 @@
         rnd.drain()
 
 
-def phase4_from(rnd, pieces, extra):
-    rnd.phase4(Pieces(pieces), extra)
-
-
-class Pieces:
-    def __init__(self, pieces):
-        self.pieces = pieces
-
-    def __getitem__(self, key):
-        return self.pieces[key[0]][key[1]]
-
-
 def on_device(
     nx, nz, ranks, py,
     field, hidden_fine, seam_tile, seam_code, corner_tile, corner_cell, pair_list, enc_weight, enc_bias,
     gru_input, gru_state, gru_bias, coarse_gain, coarse_shift, coarse_weight, dec_weight, dec_bias,
 ):
     cut = LANES // ranks
-    rows = lambda v: jnp.transpose(v[:, 0], (1, 0, 2)).reshape(ROWS, ranks, cut, LANES)
-    turn = jnp.asarray(jnp.arange(LANES)[:, None] + jnp.arange(LANES)[None, :] == LANES - 1, BF16)
-    vmem, smem, anywhere = (pl.BlockSpec(memory_space=s) for s in (pltpu.VMEM, pltpu.SMEM, pl.ANY))
+    vmem, anywhere = (pl.BlockSpec(memory_space=s) for s in (pltpu.VMEM, pl.ANY))
     slab = (ROWS, ranks, cut, LANES)
     scratch = [
         pltpu.VMEM((3, 2 * LANES, 3 * LANES), BF16),
@@ -721,30 +751,34 @@
     scratch += [pltpu.VMEM((3 * LANES, 9 * LANES), BF16)]
     scratch += [
         pltpu.VMEM((3, LANES, ROWS * LANES), F32),
-        pltpu.VMEM((2 * 3 * 2 * nx, 3, cut, LANES), BF16),
-        pltpu.SMEM((nz * 12,), jnp.int32),
+        pltpu.VMEM((2 * 3 * 2 * nx, cut, LANES), BF16),
+        pltpu.SMEM((2 * nz * 12,), jnp.int32),
         pltpu.SemaphoreType.DMA((5,)),
         pltpu.VMEM((LANES, LANES), F32),
     ]
     scratch += [pltpu.VMEM(slab, BF16) for _ in range(2)]
     scratch += [pltpu.VMEM((2, ranks, cut, LANES), BF16) for _ in range(2)]
-    scratch += [pltpu.VMEM(slab, BF16)]
-    for a, a4 in ((3, 3), (2, 3), (2, 2), (2, 3)):
+    scratch += [pltpu.VMEM(slab, BF16) for _ in range(3)] + [pltpu.VMEM((LANES, LANES), BF16)]
+    scratch += [pltpu.VMEM((LANES, ROWS, LANES), BF16)] * 2
+    scratch += [pltpu.SMEM((4, seam_tile.shape[0]), jnp.int32)] * 4 + [pltpu.SMEM(pair_list.shape, jnp.int32)]
+    scratch += [pltpu.VMEM((LANES, LANES), BF16), pltpu.VMEM((1, LANES), F32), pltpu.VMEM((3, 2, LANES), F32)]
+    scratch += [pltpu.VMEM((1, LANES), F32)] * 3 + [pltpu.SemaphoreType.DMA((13,))]
+    for a, a4 in ((2, 2), (2, 3), (2, 2), (2, 3), (2, 2)):
         scratch += round_scratch(a, a4, nx, nz, ranks, cut)
     state, memory = pl.pallas_call(
         functools.partial(kernel, (nx, nz, ranks, py)),
         out_shape=[jax.ShapeDtypeStruct(slab, BF16)] * 2,
-        in_specs=[vmem] * 2 + [smem] * 5 + [anywhere] * 4 + [vmem] * 7,
+        in_specs=[anywhere] * 17,
         out_specs=[vmem] * 2,
         scratch_shapes=scratch,
         compiler_params=pltpu.CompilerParams(
             collective_id=0, has_side_effects=True, vmem_limit_bytes=60 * 2**20
         ),
     )(
-        rows(field), rows(hidden_fine), seam_tile.T, seam_code.T, corner_tile.T, corner_cell.T, pair_list,
+        field[:, 0], hidden_fine[:, 0], seam_tile.T, seam_code.T, corner_tile.T, corner_cell.T, pair_list,
         enc_weight, gru_input, gru_state, dec_weight, coarse_weight,
         enc_bias[None], jnp.transpose(gru_bias, (1, 0, 2)), coarse_gain[None], coarse_shift[None],
-        dec_bias[None], turn,
+        dec_bias[None],
     )
     back = lambda v: jnp.transpose(v.reshape(ROWS, LANES, LANES), (1, 0, 2))[:, None]
     return back(state), back(memory)

time: 109 us -> 103 us (0.945)
  Pallas kernels: 104 us -> 101 us
  local copies, waits for them, and re-layouts: 4.16 us -> 1.87 us
    pallas_call x1, Pallas kernels: 104 us -> 101 us  [on_device(): pl.pallas_call(functools.partial(kernel, (nx, nz, ranks, py)), out_shape=...]
    transpose x2 -> x0, local copies, waits for them, and re-layouts: 2.29 us -> none  [on_device(): jnp.transpose(v[:, 0], (1, 0, 2)).reshape(ROWS, ranks, cut, LANES)]
where the time goes in v2:
time: 103 us
  Pallas kernels  101 us (98%)
  local copies, waits for them, and re-layouts  1.87 us (2%)
    pallas_call x1, Pallas kernels, on_device(): pl.pallas_call(functools.partial(kernel, (nx, nz, ranks, py)), out_shape=...  101 us

profile of v2, /device:TPU:1, one launch (start us, length us, event | category | flops | bytes accessed | tf_op | source)
XLA Modules:
  0.0 103.0 jit_solution(4664759725040699412)
XLA Ops:
  0.6 100.5 %shard_map.176 = (bf16[4,8,16,128]{3,2,1,0:T(8,128)(2,1)}, bf16[4,8,16,128]{3,2,1,0:T(8,128)(2,1)}) custom-call(bf16[128,4,128]{2,1,0:T(4,128)(2,1)} %bitcast.21, bf16[128,4,128]{2,1,0:T(4,128)(2,1)} %bitcast.22, s32[4,32]{1,0:T(4,128)} %bitcast.26, s32[4,32]{1,0:T(4,128)} %bitcast.27, s32[4,32]{1,0:T(4,128)} %bitcast.28, s32[4,32]{1,0:T(4,128)} %bitcast.29, ...), custom_call_target="tpu_custom_call" | custom-call | tf_op jit(solution)/shard_map/pallas_call | solution.py:768
  101.1 1.9 %copy_bitcast_fusion = (bf16[128,1,4,128]{3,2,1,0:T(4,128)(2,1)}, bf16[128,1,4,128]{3,2,1,0:T(4,128)(2,1)}) fusion(bf16[4,128,128]{2,1,0:T(8,128)(2,1)} %bitcast.24, bf16[4,128,128]{2,1,0:T(8,128)(2,1)} %bitcast.23), kind=kLoop, calls=%fused_computation | loop fusion | bytes 524288 | tf_op jit(solution)/shard_map/broadcast_in_dim | solution.py:783

commit v3 on v2

--- a/solution.py
+++ b/solution.py
@@ -58,12 +58,19 @@
         self.i = self.x * 2 + self.k
         self.lines = 2 * nx
 
+    def far_first(self):
+        half = self.ranks // 2
+        return sorted(range(1, self.ranks), key=lambda d: abs(d - half))
+
     def chan_peer(self, d):
         return lax.rem(self.c + d, self.ranks)
 
     def line_peer(self, d):
         other = lax.rem(self.i + d, self.lines)
         return lax.div(other, 2) * (2 * self.nz) + self.z * 2 + lax.rem(other, 2)
+
+    def x_peer(self, dx, k):
+        return lax.rem(self.x + dx, self.nx) * (2 * self.nz) + self.z * 2 + k
 
     def z_peer(self, d):
         z, k = lax.rem(self.z + d // 2, self.nz), lax.rem(self.k + d % 2, 2)
@@ -91,17 +98,17 @@
         lanes = lane_ids(LANES)
         for a, (rows, deep) in enumerate(self.arrays):
             each = ROWS // rows.shape[0]
-            tile = jnp.zeros((LANES, LANES), F32)
+            tile = jnp.zeros((LANES, LANES), BF16)
             for q in range(ROWS):
-                row = flat(rows[q // each]).astype(F32)
+                row = flat(rows[q // each])
                 tile = jnp.where(lanes == q, row[:, deep : deep + 1], tile)
                 tile = jnp.where(lanes == LANES - py + q, row[:, LANES - 1 - deep : LANES - deep], tile)
             tile = pltpu.roll(tile, ROWS * at.c, 1)
             if sums is not None and a == self.a - 1:
                 parts = three_parts(sums[0]) + three_parts(sums[1])
                 for j, part in enumerate(parts):
-                    tile = jnp.where(lanes == py + 6 * at.c + j, part, tile)
-            self.cols_src[:, a] = tile.astype(BF16).reshape(ranks, -1, LANES)
+                    tile = jnp.where(lanes == py + 6 * at.c + j, part.astype(BF16), tile)
+            self.cols_src[:, a] = tile.reshape(ranks, -1, LANES)
 
     def phase1(self, columns=None):
         at, ranks = self.at, self.at.ranks
@@ -133,7 +140,7 @@
         if columns is not None:
             columns()
         self.local(self.cols_src.at[at.c], self.p1.at[at.c], 0).start()
-        for d in range(1, ranks):
+        for d in at.far_first():
             to = at.chan_peer(d)
             self.remote(self.cols_src.at[to], self.p1.at[at.c], 0, 0, at.t, to).start()
 
@@ -143,10 +150,11 @@
         for a in range(self.a):
             self.own[a, 0] = self.p1[ranks, a]
             self.own[a, 1] = self.p1[ranks + 1, a]
-            merged = self.p1[0, a].astype(F32)
+            merged = self.p1[0, a]
             for r in range(1, ranks):
-                merged = merged + self.p1[r, a].astype(F32)
+                merged = merged + self.p1[r, a]
             if sums and a == self.a - 1:
+                merged = merged.astype(F32)
                 lanes = lane_ids(merged.shape[0])
                 held = (lanes >= py) & (lanes < py + 6 * ranks)
                 kind = lax.rem(lanes - py + 6 * LANES, 6) < 3
@@ -159,10 +167,16 @@
                 for j, part in enumerate(parts):
                     merged = jnp.where(lanes == py + 6 * at.i + j, part, merged)
             self.own[a, 2] = merged.astype(BF16)
-        self.local(self.own.at[at.k], self.r8.at[at.i], 1).start()
-        for d in range(1, at.lines):
-            to = at.line_peer(d)
-            self.remote(self.own.at[lax.rem(to, 2)], self.r8.at[at.i], 5, 1, to, at.c).start()
+            for dx in sorted(range(1, at.nx), key=lambda d: abs(2 * d - at.nx)):
+                self.remote(self.own.at[a], self.r8.at[at.i], 5, 1, at.x_peer(dx, a), at.c).start()
+
+            @pl.when(at.k == a)
+            def _():
+                self.local(self.own.at[a], self.r8.at[at.i], 1).start()
+
+            @pl.when(at.k != a)
+            def _():
+                self.remote(self.own.at[a], self.r8.at[at.i], 5, 1, at.x_peer(0, a), at.c).start()
 
     def phase3(self, both, sums=False, deep=False):
         at, py = self.at, self.py
@@ -178,23 +192,23 @@
 
         def take(d, e):
             index = self.sel[d * 12 + e]
-            value = both[jnp.maximum(index, 0)].astype(F32)
-            return jnp.where(index >= 0, value, 0.0)
+            value = both[jnp.maximum(index, 0)]
+            return jnp.where(index >= 0, value, jnp.zeros_like(value))
 
         def shift(value, by):
             return pltpu.roll(value, by % LANES, 1)
 
-        base = jnp.zeros((cut, LANES), F32)
+        base = jnp.zeros((cut, LANES), BF16)
         if sums:
-            gathered = self.r8[0, 2].astype(F32)
+            gathered = self.r8[0, 2]
             for i in range(1, at.lines):
-                gathered = gathered + self.r8[i, 2].astype(F32)
+                gathered = gathered + self.r8[i, 2]
             gathered = shift(gathered, 2 * width - py)
-            base = jnp.where((lanes >= 2 * width) & (lanes < 2 * width + 6 * at.lines), gathered, 0.0)
+            base = jnp.where((lanes >= 2 * width) & (lanes < 2 * width + 6 * at.lines), gathered, base)
 
         def partial(d, dst):
-            dst[0] = take(d, 0).astype(BF16)
-            dst[1] = take(d, 1).astype(BF16)
+            dst[0] = take(d, 0)
+            dst[1] = take(d, 1)
             tile = base
             left = shift(take(d, 2), 1 + py)
             tile = jnp.where((lanes >= 1) & (lanes <= py), left, tile)
@@ -206,10 +220,10 @@
                 if deep:
                     beside = 2 * width + e - 4
                     tile = jnp.where(lanes == beside, shift(value, beside - 1), tile)
-            dst[2] = tile.astype(BF16)
+            dst[2] = tile
 
         slot = at.z * 2 + at.k
-        for d in reversed(range(1, 2 * at.nz)):
+        for d in sorted(range(1, 2 * at.nz), key=lambda d: abs(2 * (d // 2) - at.nz)):
             partial(d, self.p3src.at[d - 1])
             self.remote(self.p3src.at[d - 1], self.p3.at[slot], 6, 2, at.z_peer(d), at.c).start()
         partial(0, self.p3.at[slot])
@@ -219,9 +233,10 @@
         total = {}
         for p in range(3):
             for a in range(self.a):
-                total[p, a] = self.p3[a, p].astype(F32)
+                value = self.p3[a, p]
                 for z in range(1, self.at.nz):
-                    total[p, a] = total[p, a] + self.p3[2 * z + a, p].astype(F32)
+                    value = value + self.p3[2 * z + a, p]
+                total[p, a] = value
         return total
 
     def phase4(self, total, extra=None):
@@ -231,10 +246,6 @@
                 self.h[p, a] = total[p, a].astype(BF16)
             if extra is not None:
                 self.h[p, self.a] = extra[p].astype(BF16)
-        self.local(self.h.at[2], self.cols.at[at.c], 5).start()
-        for d in range(1, ranks):
-            to = at.chan_peer(d)
-            self.remote(self.h.at[2], self.cols.at[at.c], 7, 5, at.t, to).start()
         for side, rank, buf, bufx, sem in ((0, 0, self.up, self.upx, 3), (1, ranks - 1, self.dn, self.dnx, 4)):
             pieces = [(self.h.at[side, a], buf.at[a, at.c], 8 + side, sem) for a in range(self.a)]
             if self.extra:
@@ -249,6 +260,11 @@
             def _():
                 for src, dst, send, recv in pieces:
                     self.remote(src, dst, send, recv, at.t, rank).start()
+
+        self.local(self.h.at[2], self.cols.at[at.c], 5).start()
+        for d in at.far_first():
+            to = at.chan_peer(d)
+            self.remote(self.h.at[2], self.cols.at[at.c], 7, 5, at.t, to).start()
 
     def finish(self):
         at = self.at
@@ -266,7 +282,7 @@
                 wait_for(self.dnx, self.recv.at[7])
 
     def slab_cols(self, a):
-        value = flat(self.cols[:, a]).astype(F32)
+        value = flat(self.cols[:, a])
         return pltpu.roll(value, lax.rem(LANES - ROWS * self.at.c, LANES), 1)
 
     def drain(self):
@@ -320,21 +336,23 @@
 
 def put_rows(stack, rows, cols, left_lane, right_lane, slots=None):
     lanes = lane_ids(LANES)
+    cols = cols.astype(BF16)
+    held = {}
     for q, row in enumerate(rows):
-        wide = row.astype(F32)
         here = pl.ds((q if slots is None else slots[q]) * LANES, LANES)
         first, last = left_lane + q, right_lane + q
-        left = jnp.where(lanes == 0, cols[:, first : first + 1], pltpu.roll(wide, 1, 1))
-        right = jnp.where(lanes == LANES - 1, cols[:, last : last + 1], pltpu.roll(wide, LANES - 1, 1))
-        stack[pl.ds(0, LANES), here] = left.astype(BF16)
-        stack[pl.ds(LANES, LANES), here] = row.astype(BF16)
-        stack[pl.ds(2 * LANES, LANES), here] = right.astype(BF16)
+        if id(row) not in held:
+            held[id(row)] = pltpu.roll(row, 1, 1), pltpu.roll(row, LANES - 1, 1)
+        left, right = held[id(row)]
+        stack[pl.ds(0, LANES), here] = jnp.where(lanes == 0, cols[:, first : first + 1], left)
+        stack[pl.ds(LANES, LANES), here] = row
+        stack[pl.ds(2 * LANES, LANES), here] = jnp.where(lanes == LANES - 1, cols[:, last : last + 1], right)
 
 
 def deep_cols(rnd, at, rows, py):
     width = py + 2
     lanes = lane_ids(LANES)
-    near, far = flat(rnd.cols[:, 0]).astype(F32), flat(rnd.cols[:, 1]).astype(F32)
+    near, far = flat(rnd.cols[:, 0]), flat(rnd.cols[:, 1])
 
     def place(value):
         left = pltpu.roll(value, lax.rem(2 * LANES + 1 - ROWS * at.c, LANES), 1)
@@ -356,18 +374,17 @@
         two = put(two, base + 1, near, beside + n, top)
         two = put(two, base + 6, near, beside + 2 + n, bottom)
         two = put(two, base + 7, far, beside + 2 + n, bottom)
-    zero = jnp.zeros((LANES, LANES), F32)
+    zero = jnp.zeros((LANES, LANES), BF16)
     for q, row in enumerate(rows):
-        wide = row.astype(F32)
-        zero = jnp.where(lanes == q, wide[:, 0:1], zero)
-        zero = jnp.where(lanes == HALF + q, wide[:, LANES - 1 :], zero)
+        zero = jnp.where(lanes == q, row[:, 0:1], zero)
+        zero = jnp.where(lanes == HALF + q, row[:, LANES - 1 :], zero)
     return zero, one, two
 
 
 def edge_stack(edge, rows, cols, open_vertex):
     zero, one, two = cols
     lanes = lane_ids(LANES)
-    hide = lambda tile, lane, n: jnp.where(lanes == jnp.where(open_vertex[n], lane, -1), 0.0, tile)
+    hide = lambda tile, lane, n: jnp.where(lanes == jnp.where(open_vertex[n], lane, -1), jnp.zeros_like(tile), tile)
     upper = hide(hide(one, 2, 0), HALF + 2, 1)
     lower = hide(hide(one, 5, 2), HALF + 5, 3)
     put_rows(edge, rows[:3], upper, 0, HALF, (0, 3, 6))
@@ -388,7 +405,7 @@
                 tile = hide(tile, 4, 2)
             if a == 2 and b == 0:
                 tile = hide(tile, HALF + 4, 3)
-            edge[pl.ds(b * LANES, LANES), pl.ds((3 * a + 2) * LANES, LANES)] = tile.astype(BF16)
+            edge[pl.ds(b * LANES, LANES), pl.ds((3 * a + 2) * LANES, LANES)] = tile
 
 
 def conv_rows(stack, weight, row, gates=None):
@@ -509,7 +526,7 @@
 
     def close_vertices(cols, left, right):
         for n, lane in enumerate((left, right, left + ROWS + 1, right + ROWS + 1)):
-            cols = jnp.where(lanes == jnp.where(open_vertex[n], lane, -1), 0.0, cols)
+            cols = jnp.where(lanes == jnp.where(open_vertex[n], lane, -1), jnp.zeros_like(cols), cols)
         return cols
 
     def stack_rows(rows, rnd, a, stack, vertices=False):
@@ -660,7 +677,7 @@
 
         extra = []
         for side in range(2):
-            value = norm(total[side, 1], *stats[side])
+            value = norm(total[side, 1].astype(F32), *stats[side])
             extra.append(jnp.where(seams[side] >= 0, value, 0.0))
         average = jnp.zeros((cut, LANES), F32)
         scale = jnp.zeros((cut, LANES), F32)
@@ -672,10 +689,10 @@
             scale = jnp.where(inside, stats[e][1], scale)
             flag = jnp.where((seams + corners)[e] >= 0, 1.0, 0.0)
             valid = jnp.where(inside, flag, valid)
-        extra.append(jnp.where(valid > 0.0, norm(total[2, 1], average, scale), 0.0))
+        extra.append(jnp.where(valid > 0.0, norm(total[2, 1].astype(F32), average, scale), 0.0))
         colour = total[2, 1]
         for j, part in enumerate(three_parts(own[0]) + three_parts(own[1])):
-            colour = jnp.where(thin == 2 * width + j, part, colour)
+            colour = jnp.where(thin == 2 * width + j, part.astype(BF16), colour)
         total[2, 1] = colour
         rnd.phase4(total, extra)
         rnd.finish()
@@ -691,15 +708,15 @@
             wide(coarse_rows[0]),
             wide(coarse_rows[1]),
             jnp.where(last_rank, flat(rnd.dnx[...]).astype(F32), wide(bottom)),
-            rnd.slab_cols(2),
+            rnd.slab_cols(2).astype(F32),
         ]
-        base = [top, coarse_rows[0], coarse_rows[1], bottom, rnd.slab_cols(1)]
+        base = [top, coarse_rows[0], coarse_rows[1], bottom, rnd.slab_cols(1).astype(F32)]
         lifted = [
             (b + jnp.dot(r["mix_w"][...], v.astype(BF16), preferred_element_type=F32)).astype(BF16)
             for b, v in zip(base, active)
         ]
         body = [lifted[0], lifted[1], lifted[1], lifted[2], lifted[2], lifted[3]]
-        put_rows(s_lift, body, lifted[4].astype(F32), 0, width)
+        put_rows(s_lift, body, lifted[4], 0, width)
         stack_rows(fresh, rnd, 0, s_mem)
 
         if step == 0:

time: 103 us -> 102 us (level)
  Pallas kernels: 101 us -> 99.8 us
where the time goes in v3:
time: 102 us
  Pallas kernels  99.8 us (98%)
  local copies, waits for them, and re-layouts  1.87 us (2%)
    pallas_call x1, Pallas kernels, on_device(): pl.pallas_call(functools.partial(kernel, (nx, nz, ranks, py)), out_shape=...  99.8 us

profile of v3, /device:TPU:1, one launch (start us, length us, event | category | flops | bytes accessed | tf_op | source)
XLA Modules:
  0.0 102.3 jit_solution(5977236929264676259)
XLA Ops:
  0.6 99.8 %shard_map.176 = (bf16[4,8,16,128]{3,2,1,0:T(8,128)(2,1)}, bf16[4,8,16,128]{3,2,1,0:T(8,128)(2,1)}) custom-call(bf16[128,4,128]{2,1,0:T(4,128)(2,1)} %bitcast.21, bf16[128,4,128]{2,1,0:T(4,128)(2,1)} %bitcast.22, s32[4,32]{1,0:T(4,128)} %bitcast.26, s32[4,32]{1,0:T(4,128)} %bitcast.27, s32[4,32]{1,0:T(4,128)} %bitcast.28, s32[4,32]{1,0:T(4,128)} %bitcast.29, ...), custom_call_target="tpu_custom_call" | custom-call | tf_op jit(solution)/shard_map/pallas_call | solution.py:785
  100.4 1.9 %copy_bitcast_fusion = (bf16[128,1,4,128]{3,2,1,0:T(4,128)(2,1)}, bf16[128,1,4,128]{3,2,1,0:T(4,128)(2,1)}) fusion(bf16[4,128,128]{2,1,0:T(8,128)(2,1)} %bitcast.24, bf16[4,128,128]{2,1,0:T(8,128)(2,1)} %bitcast.23), kind=kLoop, calls=%fused_computation | loop fusion | bytes 524288 | tf_op jit(solution)/shard_map/broadcast_in_dim | solution.py:800

commit v4 on v3

--- a/solution.py
+++ b/solution.py
@@ -789,7 +789,7 @@
         out_specs=[vmem] * 2,
         scratch_shapes=scratch,
         compiler_params=pltpu.CompilerParams(
-            collective_id=0, has_side_effects=True, vmem_limit_bytes=60 * 2**20
+            collective_id=0, has_side_effects=True, vmem_limit_bytes=107 * 2**19
         ),
     )(
         field[:, 0], hidden_fine[:, 0], seam_tile.T, seam_code.T, corner_tile.T, corner_cell.T, pair_list,

time: 102 us -> 102 us (level)
  Pallas kernels: 99.8 us -> 98.7 us
    unnamed x0 -> x22, local copies, waits for them, and re-layouts: none -> 1.5 us
    pallas_call x1, Pallas kernels: 99.8 us -> 98.7 us  [on_device(): pl.pallas_call(functools.partial(kernel, (nx, nz, ranks, py)), out_shape=...]
where the time goes in v4:
time: 102 us
  Pallas kernels  98.7 us (97%)
  local copies, waits for them, and re-layouts  2.4 us (2%)
    pallas_call x1, Pallas kernels, on_device(): pl.pallas_call(functools.partial(kernel, (nx, nz, ranks, py)), out_shape=...  98.7 us

profile of v4, /device:TPU:1, one launch (start us, length us, event | category | flops | bytes accessed | tf_op | source)
XLA Modules:
  0.0 101.8 jit_solution(8635884836400544246)
XLA Ops:
  0.6 0.0 copy-start.10
  0.6 0.0 copy-start.6
  0.7 0.0 copy-start.7
  0.7 0.0 copy-start.8
  0.7 0.0 copy-start.9
  0.7 0.0 copy-start.5
  0.7 0.0 copy-start.4
  0.7 0.0 copy-start.3
  0.7 0.0 copy-start.1
  0.7 0.0 copy-start.2
  0.7 0.6 copy-done.10
  1.3 0.0 copy-done.6
  1.3 0.0 copy-done.7
  1.3 0.0 copy-done.8
  1.3 0.0 copy-done.9
  1.4 0.0 copy-done.5
  1.4 0.0 copy-done.4
  1.4 0.0 copy-done.3
  1.4 0.0 copy-done.1
  1.4 0.0 copy-done.2
  1.5 0.0 copy-start
  1.5 0.8 copy-done
  2.2 98.7 %shard_map.176 = (bf16[4,8,16,128]{3,2,1,0:T(8,128)(2,1)S(1)}, bf16[4,8,16,128]{3,2,1,0:T(8,128)(2,1)S(1)}) custom-call(bf16[128,4,128]{2,1,0:T(4,128)(2,1)} %bitcast.32, bf16[128,4,128]{2,1,0:T(4,128)(2,1)} %bitcast.33, s32[4,32]{1,0:T(4,128)S(1)} %bitcast.24, s32[4,32]{1,0:T(4,128)S(1)} %bitcast.25, s32[4,32]{1,0:T(4,128)S(1)} %bitcast.26, ...), custom_call_target="tpu_custom_call" | custom-call | tf_op jit(solution)/shard_map/pallas_call | solution.py:785
  100.9 0.9 copy_bitcast_fusion
Async XLA Ops:
  0.6 0.7 copy-start.10
  0.6 0.7 copy-start.6
  0.7 0.7 copy-start.7
  0.7 0.7 copy-start.8
  0.7 0.7 copy-start.9
  0.7 0.7 copy-start.5
  0.7 0.7 copy-start.4
  0.7 0.7 copy-start.3
  0.7 0.7 copy-start.1
  0.7 0.7 copy-start.2
  1.5 0.8 copy-start
